TPU v7x, 512 devices: a whole 4x4x16 slice. The times are simulated.
512 devices in a mesh: rep: 16 (over x, z_hi, core), fsdp: 32 (over z_lo, y).
Axes of the slice: x: 4, y: 4, z: 16 (z_hi: 2, z_lo: 8; z = z_hi * 8 + z_lo), core: 2. Of those that a mesh axis runs over, the one named last changes fastest.
Arguments:
- tokens_in: bfloat16 [16, 1536, 2048], P('rep', 'fsdp'), may hold values from -6 to 6
- cotangent: bfloat16 [16, 1536, 2048], P('rep', 'fsdp'), may hold values from -6 to 6
- up_weight: bfloat16 [2048, 8192], P(None, 'fsdp'), may hold values from -0.125 to 0.125
- down_weight: bfloat16 [8192, 2048], P('fsdp'), may hold values from -0.0625 to 0.0625
- up_moment: float32 [2048, 8192], P('rep', 'fsdp'), may hold values from -4 to 4
- down_moment: float32 [8192, 2048], P('fsdp', 'rep'), may hold values from -4 to 4
Outputs:
- new_up: bfloat16 [2048, 8192], P(None, 'fsdp')
- new_down: bfloat16 [8192, 2048], P('fsdp')
- new_up_moment: float32 [2048, 8192], P('rep', 'fsdp')
- new_down_moment: float32 [8192, 2048], P('fsdp', 'rep')
All inputs are finite; a program needn't handle non-finite values.
Results may differ from a plain program's by a relative error of at most 0.023.
Values may be sent and summed in bfloat16 or wider, within the bound.
A program may use at most 64 MiB of HBM per device.

v0:
```python
import jax
import jax.numpy as jnp
from jax import lax
from jax.sharding import PartitionSpec as P

inner_rate = 0.3
outer_rate = 0.7
momentum_factor = 0.9


def local(tokens_in, cotangent, up_weight, down_weight, up_moment, down_moment):
    pieces = (
        lax.all_gather(tokens_in, "fsdp", axis=1, tiled=True),
        lax.all_gather(cotangent, "fsdp", axis=1, tiled=True),
    )
    rows_in = pieces[0].reshape((-1, pieces[0].shape[-1]))
    rows_back = pieces[1].reshape((-1, pieces[1].shape[-1]))
    pre = jnp.dot(rows_in, up_weight, preferred_element_type=jnp.float32)
    act = jax.nn.silu(pre).astype(jnp.bfloat16)
    back = jnp.dot(rows_back, down_weight.T, preferred_element_type=jnp.float32)
    sig = jax.nn.sigmoid(pre)
    dpre = (back * sig * (1.0 + pre * (1.0 - sig))).astype(jnp.bfloat16)
    grad_up = jnp.dot(rows_in.T, dpre, preferred_element_type=jnp.float32)
    grad_down = jnp.dot(act.T, rows_back, preferred_element_type=jnp.float32)
    grad_up, grad_down = (grad_up, grad_down)
    delta_up = (inner_rate * grad_up).astype(jnp.bfloat16).astype(jnp.float32)
    delta_down = (inner_rate * grad_down).astype(jnp.bfloat16).astype(jnp.float32)
    replicas = lax.axis_size("rep")
    place = lax.axis_index("rep")
    share_rows = up_moment.shape[0]
    share_cols = down_moment.shape[1]
    total_up, total_down = (
        lax.psum(delta_up.astype(jnp.bfloat16), "rep").astype(jnp.float32),
        lax.psum(delta_down.astype(jnp.bfloat16), "rep").astype(jnp.float32),
    )
    mean_up = total_up / replicas
    mean_down = total_down / replicas
    full_up_moment, full_down_moment = (
        lax.all_gather(up_moment.astype(jnp.bfloat16), "rep", axis=0, tiled=True).astype(
            up_moment.dtype
        ),
        lax.all_gather(down_moment.astype(jnp.bfloat16), "rep", axis=1, tiled=True).astype(
            down_moment.dtype
        ),
    )
    whole_up_moment = momentum_factor * full_up_moment + mean_up
    whole_down_moment = momentum_factor * full_down_moment + mean_down
    new_up = (
        up_weight.astype(jnp.float32) - outer_rate * (mean_up + momentum_factor * whole_up_moment)
    ).astype(jnp.bfloat16)
    new_down = (
        down_weight.astype(jnp.float32)
        - outer_rate * (mean_down + momentum_factor * whole_down_moment)
    ).astype(jnp.bfloat16)
    new_up_moment = lax.dynamic_slice_in_dim(whole_up_moment, place * share_rows, share_rows, 0)
    new_down_moment = lax.dynamic_slice_in_dim(whole_down_moment, place * share_cols, share_cols, 1)
    return (new_up, new_down, new_up_moment, new_down_moment)


def solution(mesh):
    return jax.shard_map(
        local,
        mesh=mesh,
        in_specs=(
            P("rep", "fsdp", None),
            P("rep", "fsdp", None),
            P(None, "fsdp"),
            P("fsdp", None),
            P("rep", "fsdp"),
            P("fsdp", "rep"),
        ),
        out_specs=(P(None, "fsdp"), P("fsdp", None), P("rep", "fsdp"), P("fsdp", "rep")),
        check_vma=False,
    )
```

profile of v0, /device:TPU:1, one launch (start us, length us, event | category | flops | bytes accessed | tf_op | source)
XLA Modules:
  0.0 969.2 jit_solution(4210688916225091351)
XLA Ops:
  7.2 0.0 all-gather.7.cloned.1.call-start
  7.2 0.7 all-gather.7.cloned.1.call-update
  7.9 0.0 all-gather.5.cloned.1.call-start
  7.9 0.7 all-gather.5.cloned.1.call-update
  8.6 0.0 all-gather.9.cloned.1.call-start
  8.7 1.6 copy.11
  10.4 0.0 all-reduce.3.cloned.1.call-start
  10.4 219.9 %all-gather.7.cloned.1.call-done = bf16[1,1536,2048]{2,1,0:T(8,128)(2,1)} async-done(((bf16[1,48,2048]{2,1,0:T(8,128)(2,1)}), bf16[1,1536,2048]{2,1,0:T(8,128)(2,1)}) %all-gather.7.cloned.1.call-update) | async-done | bytes 6291472 | tf_op jit(solution)/shard_map/all_gather | solution.py:13
  230.4 4.8 fusion.2
  235.2 228.8 %all-gather.5.cloned.1.call-done = bf16[1,1536,2048]{2,1,0:T(8,128)(2,1)} async-done(((bf16[1,48,2048]{2,1,0:T(8,128)(2,1)}), bf16[1,1536,2048]{2,1,0:T(8,128)(2,1)}) %all-gather.5.cloned.1.call-update) | async-done | bytes 6291472 | tf_op jit(solution)/shard_map/all_gather | solution.py:14
  464.0 5.6 fusion.23
  469.6 12.3 %fusion.29 = bf16[2048,256]{0,1:T(8,128)(2,1)} fusion(bf16[1,1536,2048]{2,1,0:T(8,128)(2,1)} %all-gather.7.cloned.1.call-done, bf16[256,2048]{1,0:T(8,128)(2,1)S(1)} %copy-done.1, bf16[1,1536,2048]{2,1,0:T(8,128)(2,1)} %all-gather.5.cloned.1.call-done, f32[1536,256]{1,0:T(8,128)S(1)} %fusion.2), kind=kOutput, calls=%fused_computation.15 | convolution fusion | flops 3225812992 | bytes 16252928 | tf_op jit(solution)/shard_map/dot_general | solution.py:23
  481.9 0.0 all-gather.11.cloned.1.call-start
  482.0 0.8 copy-done.2
  482.8 0.6 convert_element_type.61
  483.5 0.6 copy.10
  484.1 77.7 %all-gather.9.cloned.1.call-done = bf16[2048,256]{0,1:T(8,128)(2,1)} async-done(((bf16[128,256]{0,1:T(8,128)(2,1)}), bf16[2048,256]{0,1:T(8,128)(2,1)}) %all-gather.9.cloned.1.call-update) | async-done | bytes 1048592 | tf_op jit(solution)/shard_map/all_gather | solution.py:39
  561.8 308.4 %all-reduce.3.cloned.1.call-done = (bf16[2048,256]{0,1:T(8,128)(2,1)}, bf16[256,2048]{1,0:T(8,128)(2,1)}) async-done(((bf16[2048,256]{0,1:T(8,128)(2,1)}, bf16[256,2048]{1,0:T(8,128)(2,1)}), (bf16[2048,256]{0,1:T(8,128)(2,1)}, bf16[256,2048]{1,0:T(8,128)(2,1)})) %all-reduce.3.cloned.1.call-update) | async-done | bytes 2097168 | tf_op jit(solution)/shard_map/psum | solution.py:33
  870.2 2.3 multiply_add_fusion.1
  872.5 0.8 copy.13
  873.3 84.2 %all-gather.11.cloned.1.call-done = bf16[256,2048]{1,0:T(8,128)(2,1)} async-done(((bf16[256,128]{1,0:T(8,128)(2,1)}), bf16[256,2048]{1,0:T(8,128)(2,1)}) %all-gather.11.cloned.1.call-update) | async-done | bytes 1048592 | tf_op jit(solution)/shard_map/all_gather | solution.py:42
  957.5 3.2 multiply_add_fusion
  960.7 0.7 constant_dynamic-slice_fusion
  961.4 1.3 copy.12
  (9 shorter events, 0.1 us)
Async XLA Ops:
  7.2 223.2 %all-gather.7.cloned.1.call-start = ((), (), s32[]{:S(2)}) async-start(), calls=%async_computation.1 | async-start | bytes 6488064 | tf_op jit(solution)/shard_map/all_gather | solution.py:13
  7.9 456.1 %all-gather.5.cloned.1.call-start = ((), (), s32[]{:S(2)}) async-start(), calls=%async_computation | async-start | bytes 6488064 | tf_op jit(solution)/shard_map/all_gather | solution.py:14
  8.6 553.1 %all-gather.9.cloned.1.call-start = ((), (), s32[]{:S(2)}) async-start(), calls=%async_computation.2 | async-start | bytes 1114112 | tf_op jit(solution)/shard_map/all_gather | solution.py:39
  10.4 859.9 %all-reduce.3.cloned.1.call-start = ((), (), s32[]{:S(2)}) async-start(), calls=%async_computation.4 | async-start | bytes 4194304 | tf_op jit(solution)/shard_map/psum | solution.py:33
  235.2 234.4 %copy-start.1 = (bf16[256,2048]{1,0:T(8,128)(2,1)S(1)}, bf16[256,2048]{1,0:T(8,128)(2,1)}, u32[]{:S(2)}) copy-start(bf16[256,2048]{1,0:T(8,128)(2,1)} %param.9) | copy-start | bytes 3145732
  481.9 0.9 copy-start.2
  481.9 1.6 copy-start
  481.9 475.6 %all-gather.11.cloned.1.call-start = ((), (), s32[]{:S(2)}) async-start(), calls=%async_computation.3 | async-start | bytes 1114112 | tf_op jit(solution)/shard_map/all_gather | solution.py:42
Sparse Core Ops, SparseCore 0:
  10.1 220.2 all-gather.6
  232.4 231.5 all-gather.4
  467.7 94.0 all-gather.8
  565.2 304.9 all-reduce.2
  873.2 84.2 all-gather.10
where the time goes:
time: 969 us
  waiting for transfers between devices  920 us (95%)
  matrix products  22.7 us (2%)
  between operations  13.8 us (1%)
    psum x1, waiting for transfers between devices, local(): lax.psum(delta_up.astype(jnp.bfloat16), 'rep').astype(jnp.float32)  308 us
    all_gather x1, waiting for transfers between devices, local(): lax.all_gather(cotangent, 'fsdp', axis=1, tiled=True)  229 us
    all_gather x1, waiting for transfers between devices, local(): lax.all_gather(tokens_in, 'fsdp', axis=1, tiled=True)  220 us
    all_gather x1, waiting for transfers between devices, local(): lax.all_gather(down_moment.astype(jnp.bfloat16), 'rep', axis=1, tiled=True)  84.2 us
    all_gather x1, waiting for transfers between devices, local(): lax.all_gather(up_moment.astype(jnp.bfloat16), 'rep', axis=0, tiled=True)  77.7 us
  transfers between devices with their start and end apart: 5, of which 5 were waited for; matrix products, arithmetic and copies ran while one was open for 3% of the time, Pallas kernels for 0%

commit v1 on v0

v1 whole, which is shorter than its diff:
```python
import functools

import jax
import jax.numpy as jnp
from jax import lax
from jax.experimental import pallas as pl
from jax.experimental.pallas import tpu as pltpu
from jax.sharding import PartitionSpec as P

inner_rate = 0.3
outer_rate = 0.7
momentum_factor = 0.9

MESH = pl.DeviceIdType.MESH
F32 = jnp.float32
BF16 = jnp.bfloat16

ROWS = 48
SLAB = 4 * ROWS
D = 2048
FL = 256
Q4 = D // 4


def device(x, zhi, core, zlo, y):
    return {"rep": (x * 2 + zhi) * 2 + core, "fsdp": zlo * 4 + y}


def outer_round(
    tok, cot, up, down, mu, md,
    o_up, o_dn, o_mu, o_md,
    X, G, Wu, Wd, accU, accD, dT, aT, sb, rb, ys, yr, cs, cb, zr, us, ds, muv, mdv,
    ld, sxz, rxz, sgz, rgz, sxy, rxy, sgy, rgy, sxc, rxc, sgc, rgc, sw, rw,
    sx, rx, sy, ry, sc, rc, sz, rz, sA, rA, sC, rC,
):
    rep = lax.axis_index("rep")
    fs = lax.axis_index("fsdp")
    x, zhi, core = rep // 4, (rep // 2) % 2, rep % 2
    zlo, y = fs // 4, fs % 4
    z = zhi * 8 + zlo
    sgn = 1 - 2 * core

    def at_z(zz):
        zz = (zz + 32) % 16
        return device(x, zz // 8, core, zz % 8, y)

    def at_x(xx):
        return device((xx + 8) % 4, zhi, core, zlo, y)

    to_long = at_z(z + sgn)
    to_short = at_z(z - sgn)
    to_pair = device(x, zhi, core, zlo, y + 1 - 2 * (y % 2))
    to_slice = device(x, zhi, core, zlo, 3 - y)
    to_core = device(x, zhi, 1 - core, zlo, y)
    to_right = at_x(x + 1)
    to_left = at_x(x - 1)
    to_zhi = device(x, 1 - zhi, core, zlo, y)
    home = (y % 2) == core

    def local(src, dst, sem):
        return pltpu.make_async_copy(src, dst, sem)

    def remote(src, dst, ssem, rsem, to):
        return pltpu.make_async_remote_copy(
            src_ref=src, dst_ref=dst, send_sem=ssem, recv_sem=rsem,
            device_id=to, device_id_type=MESH,
        )

    def slot(buf, zi, yi, ci):
        return buf.at[pl.ds(zi * SLAB + (yi * 2 + ci) * ROWS, ROWS), :]

    share_row = pl.multiple_of(rep * 128, 128)
    loads = [
        local(tok, slot(X, 0, 0, 0), ld.at[0]),
        local(cot, slot(G, 0, 0, 0), ld.at[1]),
        local(up.at[pl.ds(share_row, 128), :], us, ld.at[2]),
        local(down.at[:, pl.ds(share_row, 128)], ds, ld.at[3]),
        local(mu, muv, ld.at[4]),
        local(md, mdv, ld.at[5]),
    ]
    for c in loads:
        c.start()

    barrier = pltpu.get_barrier_semaphore()
    everyone = (to_long, to_short, to_pair, to_slice, to_core, to_right, to_left, to_zhi)
    for other in everyone:
        pl.semaphore_signal(barrier, inc=1, device_id=other, device_id_type=MESH)
    loads[0].wait()
    loads[1].wait()
    pl.semaphore_wait(barrier, len(everyone))

    sent = []

    def go(copy):
        copy.start()
        sent.append(copy)

    def x_z(src_zi, dst_zi, to):
        return remote(slot(X, src_zi, 0, 0), slot(X, dst_zi, 0, 0), sxz.at[dst_zi], rxz.at[dst_zi], to)

    def g_z(src_zi, dst_zi, yi, to):
        return remote(
            slot(G, src_zi, yi, 0), slot(G, dst_zi, yi, 0), sgz.at[dst_zi, yi], rgz.at[dst_zi, yi], to
        )

    def x_y(zi):
        return remote(slot(X, zi, 0, 0), slot(X, zi, 1, 0), sxy.at[zi], rxy.at[zi], to_pair)

    def g_y():
        return remote(slot(G, 0, 0, 0), slot(G, 0, 1, 0), sgy.at[0], rgy.at[0], to_pair)

    def x_c(zi, yi):
        return remote(slot(X, zi, yi, 0), slot(X, zi, yi, 1), sxc.at[zi, yi], rxc.at[zi, yi], to_core)

    def g_c(zi, yi):
        return remote(slot(G, zi, yi, 0), slot(G, zi, yi, 1), sgc.at[zi, yi], rgc.at[zi, yi], to_core)

    go(g_y())
    go(x_z(0, 1, to_long))
    go(x_z(0, 2, to_short))
    go(g_z(0, 1, 0, to_long))
    go(g_z(0, 2, 0, to_short))
    go(x_y(0))
    go(x_c(0, 0))
    go(g_c(0, 0))

    w_send = [
        remote(up, Wu, sw.at[0], rw.at[0], to_slice),
        remote(down, Wd, sw.at[1], rw.at[1], to_slice),
    ]
    w_local = [local(up, Wu, ld.at[6]), local(down, Wd, ld.at[7])]

    @pl.when(home)
    def _():
        for c in w_send + w_local:
            c.start()

    g_y().wait_recv()
    go(g_z(0, 1, 1, to_long))
    go(g_z(0, 2, 1, to_short))
    go(g_c(0, 1))
    x_y(0).wait_recv()
    go(x_c(0, 1))

    def arrived_x(zi, onward, to):
        x_z(0, zi, to_long).wait_recv()
        if onward:
            go(x_z(zi, zi + 2, to))
        go(x_y(zi))
        go(x_c(zi, 0))

    def arrived_g(zi, yi, onward, to):
        g_z(0, zi, yi, to_long).wait_recv()
        if onward:
            go(g_z(zi, zi + 2, yi, to))
        go(g_c(zi, yi))

    def arrived_pair(zi):
        x_y(zi).wait_recv()
        go(x_c(zi, 1))

    for k in (1, 2, 3):
        long, short = 2 * k - 1, 2 * k
        arrived_x(long, True, to_long)
        arrived_x(short, k < 3, to_short)
        arrived_g(long, 0, True, to_long)
        arrived_g(short, 0, k < 3, to_short)
        arrived_pair(long)
        arrived_pair(short)
        arrived_g(long, 1, True, to_long)
        arrived_g(short, 1, k < 3, to_short)

    def from_core(zi):
        for yi in (0, 1):
            x_c(zi, yi).wait_recv()
            g_c(zi, yi).wait_recv()

    def middle(row, n):
        rows = pl.ds(row, n)
        pre = jnp.dot(X[rows, :], Wu[...], preferred_element_type=F32)
        back = lax.dot_general(G[rows, :], Wd[...], (((1,), (1,)), ((), ())), preferred_element_type=F32)
        s = jax.nn.sigmoid(pre)
        act = pre * s
        dpre = back * s * (1.0 + pre * (1.0 - s))
        dT[:, :n] = dpre.T.astype(BF16)
        aT[:, :n] = act.T.astype(BF16)

    def grads(row, n, first):
        rows = pl.ds(row, n)

        @pl.loop(0, D // 256)
        def _(j):
            cols = pl.ds(pl.multiple_of(j * 256, 256), 256)
            du = jnp.dot(dT[:, :n], X[rows, cols], preferred_element_type=F32)
            dd = jnp.dot(aT[:, :n], G[rows, cols], preferred_element_type=F32)
            accU[:, cols] = du if first else accU[:, cols] + du
            accD[:, cols] = dd if first else accD[:, cols] + dd

    @pl.when(home)
    def _():
        for c in w_local:
            c.wait()

    @pl.when(jnp.logical_not(home))
    def _():
        for c in w_send:
            c.wait_recv()

    from_core(0)
    middle(0, SLAB)
    grads(0, SLAB, True)
    for k in (1, 2):
        from_core(2 * k - 1)
        from_core(2 * k)
        middle((2 * k - 1) * SLAB, 2 * SLAB)
        grads((2 * k - 1) * SLAB, 2 * SLAB, False)

    arrived_x(7, False, to_long)
    from_core(5)
    from_core(6)
    middle(5 * SLAB, 2 * SLAB)
    grads(5 * SLAB, 2 * SLAB, False)
    arrived_g(7, 0, False, to_long)
    arrived_pair(7)
    arrived_g(7, 1, False, to_long)
    from_core(7)
    middle(7 * SLAB, SLAB)

    last = pl.ds(7 * SLAB, SLAB)

    def quarter(step):
        return pl.ds(pl.multiple_of(((x + step) % 4) * Q4, Q4), Q4)

    def total_up(cols):
        return accU[:, cols] + jnp.dot(dT[:, :SLAB], X[last, cols], preferred_element_type=F32)

    def total_dn(cols):
        return accD[:, cols] + jnp.dot(aT[:, :SLAB], G[last, cols], preferred_element_type=F32)

    def x_sum(i):
        return remote(sb.at[i], rb.at[i], sx.at[i], rx.at[i], to_right if i % 2 == 0 else to_left)

    sb[0] = total_up(quarter(2)).astype(BF16)
    go(x_sum(0))
    sb[1] = total_dn(quarter(2)).astype(BF16)
    go(x_sum(1))
    sb[2] = total_dn(quarter(1)).astype(BF16)
    go(x_sum(2))
    sb[3] = total_up(quarter(3)).astype(BF16)
    go(x_sum(3))
    accU[:, quarter(1)] = total_up(quarter(1))
    accD[:, quarter(3)] = total_dn(quarter(3))
    x_sum(0).wait_recv()
    sb[4] = (accU[:, quarter(1)] + rb[0].astype(F32)).astype(BF16)
    go(x_sum(4))
    x_sum(1).wait_recv()
    sb[5] = (accD[:, quarter(3)] + rb[1].astype(F32)).astype(BF16)
    go(x_sum(5))
    accU[:, quarter(0)] = total_up(quarter(0))
    accD[:, quarter(0)] = total_dn(quarter(0))
    for i in (2, 3, 4, 5):
        x_sum(i).wait_recv()

    def part(a, off, width):
        cols = pl.ds(pl.multiple_of(x * Q4 + off, 128), width)
        here = pl.ds(pl.multiple_of(off, 128), width)
        if a == 0:
            return accU[:, cols] + rb[3, :, here].astype(F32) + rb[4, :, here].astype(F32)
        return accD[:, cols] + rb[2, :, here].astype(F32) + rb[5, :, here].astype(F32)

    def y_sum(a):
        return remote(ys.at[a], yr.at[a], sy.at[a], ry.at[a], to_slice)

    def c_sum(h, a):
        return remote(cs.at[h, a], cb.at[h, a], sc.at[h, a], rc.at[h, a], to_core)

    @pl.when(jnp.logical_not(home))
    def _():
        for a in (0, 1):
            ys[a] = part(a, 0, Q4).astype(BF16)
            y_sum(a).start()
        for a in (0, 1):
            for h in (0, 1):
                c_sum(h, a).wait_recv()
        for a in (0, 1):
            y_sum(a).wait_send()

    @pl.when(home)
    def _():
        for a in (0, 1):
            y_sum(a).wait_recv()
            for h in (0, 1):
                theirs = pl.multiple_of(h * 256 + (1 - core) * 128, 128)
                mine = pl.multiple_of(h * 256 + core * 128, 128)
                cs[h, a] = (part(a, theirs, 128) + yr[a, :, pl.ds(theirs, 128)].astype(F32)).astype(BF16)
                c_sum(h, a).start()
                cb[h, a] = (part(a, mine, 128) + yr[a, :, pl.ds(mine, 128)].astype(F32)).astype(BF16)
        for a in (0, 1):
            for h in (0, 1):
                c_sum(h, a).wait_send()
        for c in w_send:
            c.wait_send()

    def z_sum(a):
        return remote(cb.at[1 - zhi, a], zr.at[a], sz.at[a], rz.at[a], to_zhi)

    for a in (0, 1):
        go(z_sum(a))
    for c in loads[2:]:
        c.wait()

    replicas = 16

    def spot(a, xx, zz, cc):
        at = pl.ds(pl.multiple_of(((xx * 2 + zz) * 2 + cc) * 128, 128), 128)
        return o_up.at[at, :] if a == 0 else o_dn.at[:, at]

    z_sum(0).wait_recv()
    mean = (cb[zhi, 0].astype(F32) + zr[0].astype(F32)).T * (inner_rate / replicas)
    moment = momentum_factor * muv[...] + mean
    o_mu[...] = moment
    o_up[pl.ds(share_row, 128), :] = (
        us[...].astype(F32) - outer_rate * (mean + momentum_factor * moment)
    ).astype(BF16)

    def a_z(a):
        return remote(spot(a, x, zhi, core), spot(a, x, zhi, core), sA.at[1, 0, a], rA.at[1, 0, a], to_zhi)

    def z_in(a):
        return remote(spot(a, x, zhi, core), spot(a, x, 1 - zhi, core), sA.at[1, 0, a], rA.at[1, 0, a], to_zhi)

    go(a_z(0))
    z_sum(1).wait_recv()
    mean = (cb[zhi, 1].astype(F32) + zr[1].astype(F32)) * (inner_rate / replicas)
    moment = momentum_factor * mdv[...] + mean
    o_md[...] = moment
    o_dn[:, pl.ds(share_row, 128)] = (
        ds[...].astype(F32) - outer_rate * (mean + momentum_factor * moment)
    ).astype(BF16)
    go(a_z(1))

    back_by = {0: 0, 1: 1, 2: 2, 3: -1}

    def hold(a, q, j):
        return spot(a, (x - back_by[j] + 4) % 4, (zhi + q) % 2, core)

    def a_x(a, q, j, dst_j, to):
        return remote(hold(a, q, j), hold(a, q, j), sA.at[q, dst_j, a], rA.at[q, dst_j, a], to)

    def x_in(a, q, j):
        return remote(hold(a, q, j), hold(a, q, j), sA.at[q, j, a], rA.at[q, j, a], to_right)

    def a_c(a, q, j):
        return remote(hold(a, q, j), hold(a, q, j), sC.at[q, j, a], rC.at[q, j, a], to_core)

    def c_in(a, q, j):
        there = spot(a, (x - back_by[j] + 4) % 4, (zhi + q) % 2, 1 - core)
        return remote(there, there, sC.at[q, j, a], rC.at[q, j, a], to_core)

    for q in (0, 1):
        if q == 1:
            for a in (0, 1):
                z_in(a).wait_recv()
                go(a_x(a, 1, 0, 1, to_right))
                go(a_x(a, 1, 0, 3, to_left))
                go(a_c(a, 1, 0))
        else:
            for a in (0, 1):
                go(a_x(a, 0, 0, 1, to_right))
                go(a_x(a, 0, 0, 3, to_left))
                go(a_c(a, 0, 0))
        x_in(0, q, 1).wait_recv()
        go(a_x(0, q, 1, 2, to_right))
        go(a_c(0, q, 1))
        x_in(1, q, 3).wait_recv()
        go(a_x(1, q, 3, 2, to_left))
        go(a_c(1, q, 3))
        x_in(1, q, 1).wait_recv()
        go(a_c(1, q, 1))
        x_in(0, q, 3).wait_recv()
        go(a_c(0, q, 3))
        for a in (0, 1):
            x_in(a, q, 2).wait_recv()
            go(a_c(a, q, 2))
    for q in (0, 1):
        for j in (0, 1, 2, 3):
            for a in (0, 1):
                c_in(a, q, j).wait_recv()
    for c in sent:
        c.wait_send()


def local(tokens_in, cotangent, up_weight, down_weight, up_moment, down_moment):
    dma = pltpu.SemaphoreType.DMA
    vmem = pltpu.VMEM
    return pl.pallas_call(
        outer_round,
        out_shape=(
            jax.ShapeDtypeStruct(up_weight.shape, BF16),
            jax.ShapeDtypeStruct(down_weight.shape, BF16),
            jax.ShapeDtypeStruct(up_moment.shape, F32),
            jax.ShapeDtypeStruct(down_moment.shape, F32),
        ),
        in_specs=[pl.BlockSpec(memory_space=pl.ANY)] * 6,
        out_specs=[pl.BlockSpec(memory_space=pltpu.VMEM)] * 4,
        scratch_shapes=[
            vmem((8 * SLAB, D), BF16), vmem((8 * SLAB, D), BF16),
            vmem((D, FL), BF16), vmem((FL, D), BF16),
            vmem((FL, D), F32), vmem((FL, D), F32),
            vmem((FL, 2 * SLAB), BF16), vmem((FL, 2 * SLAB), BF16),
            vmem((6, FL, Q4), BF16), vmem((6, FL, Q4), BF16),
            vmem((2, FL, Q4), BF16), vmem((2, FL, Q4), BF16),
            vmem((2, 2, FL, 128), BF16), vmem((2, 2, FL, 128), BF16),
            vmem((2, FL, 128), BF16),
            vmem((128, FL), BF16), vmem((FL, 128), BF16),
            vmem((128, FL), F32), vmem((FL, 128), F32),
            dma((8,)),
            dma((8,)), dma((8,)), dma((8, 2)), dma((8, 2)), dma((8,)), dma((8,)), dma((1,)), dma((1,)),
            dma((8, 2)), dma((8, 2)), dma((8, 2)), dma((8, 2)), dma((2,)), dma((2,)),
            dma((6,)), dma((6,)), dma((2,)), dma((2,)), dma((2, 2)), dma((2, 2)), dma((2,)), dma((2,)),
            dma((2, 4, 2)), dma((2, 4, 2)), dma((2, 4, 2)), dma((2, 4, 2)),
        ],
        compiler_params=pltpu.CompilerParams(
            collective_id=0, has_side_effects=True, vmem_limit_bytes=48 << 20
        ),
        name="outer_round",
    )(tokens_in[0], cotangent[0], up_weight, down_weight, up_moment, down_moment)


def solution(mesh):
    return jax.shard_map(
        local,
        mesh=mesh,
        in_specs=(
            P("rep", "fsdp", None),
            P("rep", "fsdp", None),
            P(None, "fsdp"),
            P("fsdp", None),
            P("rep", "fsdp"),
            P("fsdp", "rep"),
        ),
        out_specs=(P(None, "fsdp"), P("fsdp", None), P("rep", "fsdp"), P("fsdp", "rep")),
        check_vma=False,
    )
```

time: 969 us -> 155 us (0.16)
  waiting for transfers between devices: 920 us -> 0 us
  Pallas kernels: 0 us -> 145 us
  matrix products: 22.7 us -> 0 us
  between operations: 13.8 us -> 0.66 us
    all_gather x4 -> x0, waiting for transfers between devices: 611 us -> none  [the longest x1 229 us: local(): lax.all_gather(cotangent, 'fsdp', axis=1, tiled=True)]
    psum x1 -> x0, waiting for transfers between devices: 308 us -> none  [local(): lax.psum(delta_up.astype(jnp.bfloat16), 'rep').astype(jnp.float32)]
    pallas_call x0 -> x1, Pallas kernels: none -> 145 us  [local(): pl.pallas_call(outer_round, out_shape=(jax.ShapeDtypeStruct(up_weight.sha...]
    dot_general x3 -> x0, matrix products: 22.7 us -> none  [the longest x1 12.3 us: local(): grad_up = jnp.dot(rows_in.T, dpre, preferred_element_type=jnp.float32)]
  transfers between devices with their start and end apart: 5 -> 0, of which waited for: 5 -> 0; matrix products, arithmetic and copies ran while one was open for 3% -> 0% of each run, Pallas kernels for 0% -> 0%
where the time goes in v1:
time: 155 us
  Pallas kernels  145 us (94%)
  local copies, waits for them, and re-layouts  9.35 us (6%)
    pallas_call x1, Pallas kernels, local(): pl.pallas_call(outer_round, out_shape=(jax.ShapeDtypeStruct(up_weight.sha...  145 us
    unnamed x16, local copies, waits for them, and re-layouts  9.35 us

profile of v1, /device:TPU:1, one launch (start us, length us, event | category | flops | bytes accessed | tf_op | source)
XLA Modules:
  0.0 154.9 jit_solution(17766798722263892676)
XLA Ops:
  0.6 0.0 copy-start
  0.6 1.2 copy-done
  1.9 0.0 copy-start.1
  1.9 1.2 copy-done.1
  3.1 0.0 copy-start.2
  3.1 0.9 copy-done.2
  4.0 0.0 copy-start.3
  4.0 0.9 copy-done.3
  4.9 0.0 copy-start.4
  4.9 0.9 copy-done.4
  5.8 0.0 copy-start.5
  5.8 0.9 copy-done.5
  6.7 144.9 %outer_round.1 = (bf16[2048,256]{1,0:T(8,128)(2,1)S(1)}, bf16[256,2048]{1,0:T(8,128)(2,1)S(1)}, f32[128,256]{1,0:T(8,128)S(1)}, f32[256,128]{1,0:T(8,128)S(1)}) custom-call(bf16[48,2048]{1,0:T(8,128)(2,1)S(1)} %bitcast.2, bf16[48,2048]{1,0:T(8,128)(2,1)S(1)} %bitcast.3, bf16[2048,256]{1,0:T(8,128)(2,1)S(1)} %copy-done, bf16[256,2048]{1,0:T(8,128)(2,1)S(1)} %copy-done.1, ...), custom_call_target="tpu_custom_call" | custom-call | tf_op jit(solution)/shard_map/outer_round/pallas_call | solution.py:396
  151.7 1.0 copy.14
  152.6 1.0 copy.15
  153.6 0.7 copy.16
  154.3 0.7 copy.17
Async XLA Ops:
  0.6 1.2 copy-start
  1.9 1.2 copy-start.1
  3.1 0.9 copy-start.2
  4.0 0.9 copy-start.3
  4.9 0.9 copy-start.4
  5.8 0.9 copy-start.5

commit v2 on v1

--- a/solution.py
+++ b/solution.py
@@ -159,153 +159,184 @@
         x_y(zi).wait_recv()
         go(x_c(zi, 1))
 
-    for k in (1, 2, 3):
-        long, short = 2 * k - 1, 2 * k
-        arrived_x(long, True, to_long)
-        arrived_x(short, k < 3, to_short)
-        arrived_g(long, 0, True, to_long)
-        arrived_g(short, 0, k < 3, to_short)
-        arrived_pair(long)
-        arrived_pair(short)
-        arrived_g(long, 1, True, to_long)
-        arrived_g(short, 1, k < 3, to_short)
-
     def from_core(zi):
         for yi in (0, 1):
             x_c(zi, yi).wait_recv()
             g_c(zi, yi).wait_recv()
 
-    def middle(row, n):
-        rows = pl.ds(row, n)
+    def middle(zi):
+        rows = pl.ds(zi * SLAB, SLAB)
         pre = jnp.dot(X[rows, :], Wu[...], preferred_element_type=F32)
         back = lax.dot_general(G[rows, :], Wd[...], (((1,), (1,)), ((), ())), preferred_element_type=F32)
         s = jax.nn.sigmoid(pre)
         act = pre * s
         dpre = back * s * (1.0 + pre * (1.0 - s))
-        dT[:, :n] = dpre.T.astype(BF16)
-        aT[:, :n] = act.T.astype(BF16)
-
-    def grads(row, n, first):
-        rows = pl.ds(row, n)
+        dT[...] = dpre.T.astype(BF16)
+        aT[...] = act.T.astype(BF16)
+
+    def grads(zi):
+        rows = pl.ds(zi * SLAB, SLAB)
 
         @pl.loop(0, D // 256)
         def _(j):
             cols = pl.ds(pl.multiple_of(j * 256, 256), 256)
-            du = jnp.dot(dT[:, :n], X[rows, cols], preferred_element_type=F32)
-            dd = jnp.dot(aT[:, :n], G[rows, cols], preferred_element_type=F32)
-            accU[:, cols] = du if first else accU[:, cols] + du
-            accD[:, cols] = dd if first else accD[:, cols] + dd
+            du = jnp.dot(dT[...], X[rows, cols], preferred_element_type=F32)
+            dd = jnp.dot(aT[...], G[rows, cols], preferred_element_type=F32)
+            accU[:, cols] = du if zi == 0 else accU[:, cols] + du
+            accD[:, cols] = dd if zi == 0 else accD[:, cols] + dd
+
+    def unit(zi):
+        from_core(zi)
+        middle(zi)
+        grads(zi)
+
+    for k in (1, 2, 3):
+        long, short = 2 * k - 1, 2 * k
+        arrived_x(long, True, to_long)
+        arrived_x(short, k < 3, to_short)
+        if k == 3:
+
+            @pl.when(home)
+            def _():
+                for c in w_local:
+                    c.wait()
+
+            @pl.when(jnp.logical_not(home))
+            def _():
+                for c in w_send:
+                    c.wait_recv()
+
+            unit(0)
+        arrived_g(long, 0, True, to_long)
+        arrived_g(short, 0, k < 3, to_short)
+        if k == 3:
+            unit(1)
+        arrived_pair(long)
+        arrived_pair(short)
+        if k == 3:
+            unit(2)
+        arrived_g(long, 1, True, to_long)
+        arrived_g(short, 1, k < 3, to_short)
+        if k == 3:
+            unit(3)
+
+    arrived_x(7, False, to_long)
+    unit(4)
+    arrived_g(7, 0, False, to_long)
+    unit(5)
+    arrived_pair(7)
+    unit(6)
+    arrived_g(7, 1, False, to_long)
+    from_core(7)
+    middle(7)
+
+    last = pl.ds(7 * SLAB, SLAB)
+    H4 = Q4 // 2
+    half = (1 - zhi, zhi)
+
+    def cols(step, i):
+        return pl.ds(pl.multiple_of(((x + step) % 4) * Q4 + half[i] * H4, H4), H4)
+
+    def total_up(at):
+        return accU[:, at] + jnp.dot(dT[...], X[last, at], preferred_element_type=F32)
+
+    def total_dn(at):
+        return accD[:, at] + jnp.dot(aT[...], G[last, at], preferred_element_type=F32)
+
+    def x_sum(i, n):
+        return remote(
+            sb.at[i, n], rb.at[i, n], sx.at[i, n], rx.at[i, n], to_right if n % 2 == 0 else to_left
+        )
+
+    def x_first(i):
+        sb[i, 0] = total_up(cols(2, i)).astype(BF16)
+        go(x_sum(i, 0))
+        sb[i, 1] = total_dn(cols(2, i)).astype(BF16)
+        go(x_sum(i, 1))
+        sb[i, 2] = total_dn(cols(1, i)).astype(BF16)
+        go(x_sum(i, 2))
+        sb[i, 3] = total_up(cols(3, i)).astype(BF16)
+        go(x_sum(i, 3))
+
+    def x_rest(i):
+        for a, step in ((0, 1), (1, 3), (0, 0), (1, 0)):
+            if a == 0:
+                accU[:, cols(step, i)] = total_up(cols(step, i))
+            else:
+                accD[:, cols(step, i)] = total_dn(cols(step, i))
+
+    def x_relay(i):
+        x_sum(i, 0).wait_recv()
+        sb[i, 4] = (accU[:, cols(1, i)] + rb[i, 0].astype(F32)).astype(BF16)
+        go(x_sum(i, 4))
+        x_sum(i, 1).wait_recv()
+        sb[i, 5] = (accD[:, cols(3, i)] + rb[i, 1].astype(F32)).astype(BF16)
+        go(x_sum(i, 5))
+
+    def part(i, a, off, width):
+        at = pl.ds(pl.multiple_of(x * Q4 + half[i] * H4 + off, 128), width)
+        here = pl.ds(pl.multiple_of(off, 128), width)
+        if a == 0:
+            return accU[:, at] + rb[i, 3, :, here].astype(F32) + rb[i, 4, :, here].astype(F32)
+        return accD[:, at] + rb[i, 2, :, here].astype(F32) + rb[i, 5, :, here].astype(F32)
+
+    def y_sum(i, a):
+        return remote(ys.at[i, a], yr.at[i, a], sy.at[i, a], ry.at[i, a], to_slice)
+
+    def c_sum(i, a):
+        return remote(cs.at[i, a], cb.at[i, a], sc.at[i, a], rc.at[i, a], to_core)
+
+    def y_out(i):
+        for n in (2, 3, 4, 5):
+            x_sum(i, n).wait_recv()
+
+        @pl.when(jnp.logical_not(home))
+        def _():
+            for a in (0, 1):
+                ys[i, a] = part(i, a, 0, H4).astype(BF16)
+                y_sum(i, a).start()
+
+    def y_in(i):
+        @pl.when(jnp.logical_not(home))
+        def _():
+            for a in (0, 1):
+                c_sum(i, a).wait_recv()
+            for a in (0, 1):
+                y_sum(i, a).wait_send()
+
+        @pl.when(home)
+        def _():
+            for a in (0, 1):
+                y_sum(i, a).wait_recv()
+                theirs = pl.multiple_of((1 - core) * 128, 128)
+                mine = pl.multiple_of(core * 128, 128)
+                cs[i, a] = (part(i, a, theirs, 128) + yr[i, a, :, pl.ds(theirs, 128)].astype(F32)).astype(BF16)
+                c_sum(i, a).start()
+                cb[i, a] = (part(i, a, mine, 128) + yr[i, a, :, pl.ds(mine, 128)].astype(F32)).astype(BF16)
+            for a in (0, 1):
+                c_sum(i, a).wait_send()
+
+    def z_sum(a):
+        return remote(cb.at[0, a], zr.at[a], sz.at[a], rz.at[a], to_zhi)
+
+    x_first(0)
+    x_rest(0)
+    x_relay(0)
+    x_first(1)
+    x_rest(1)
+    y_out(0)
+    x_relay(1)
+    y_in(0)
+    for a in (0, 1):
+        go(z_sum(a))
+    y_out(1)
+    y_in(1)
 
     @pl.when(home)
     def _():
-        for c in w_local:
-            c.wait()
-
-    @pl.when(jnp.logical_not(home))
-    def _():
-        for c in w_send:
-            c.wait_recv()
-
-    from_core(0)
-    middle(0, SLAB)
-    grads(0, SLAB, True)
-    for k in (1, 2):
-        from_core(2 * k - 1)
-        from_core(2 * k)
-        middle((2 * k - 1) * SLAB, 2 * SLAB)
-        grads((2 * k - 1) * SLAB, 2 * SLAB, False)
-
-    arrived_x(7, False, to_long)
-    from_core(5)
-    from_core(6)
-    middle(5 * SLAB, 2 * SLAB)
-    grads(5 * SLAB, 2 * SLAB, False)
-    arrived_g(7, 0, False, to_long)
-    arrived_pair(7)
-    arrived_g(7, 1, False, to_long)
-    from_core(7)
-    middle(7 * SLAB, SLAB)
-
-    last = pl.ds(7 * SLAB, SLAB)
-
-    def quarter(step):
-        return pl.ds(pl.multiple_of(((x + step) % 4) * Q4, Q4), Q4)
-
-    def total_up(cols):
-        return accU[:, cols] + jnp.dot(dT[:, :SLAB], X[last, cols], preferred_element_type=F32)
-
-    def total_dn(cols):
-        return accD[:, cols] + jnp.dot(aT[:, :SLAB], G[last, cols], preferred_element_type=F32)
-
-    def x_sum(i):
-        return remote(sb.at[i], rb.at[i], sx.at[i], rx.at[i], to_right if i % 2 == 0 else to_left)
-
-    sb[0] = total_up(quarter(2)).astype(BF16)
-    go(x_sum(0))
-    sb[1] = total_dn(quarter(2)).astype(BF16)
-    go(x_sum(1))
-    sb[2] = total_dn(quarter(1)).astype(BF16)
-    go(x_sum(2))
-    sb[3] = total_up(quarter(3)).astype(BF16)
-    go(x_sum(3))
-    accU[:, quarter(1)] = total_up(quarter(1))
-    accD[:, quarter(3)] = total_dn(quarter(3))
-    x_sum(0).wait_recv()
-    sb[4] = (accU[:, quarter(1)] + rb[0].astype(F32)).astype(BF16)
-    go(x_sum(4))
-    x_sum(1).wait_recv()
-    sb[5] = (accD[:, quarter(3)] + rb[1].astype(F32)).astype(BF16)
-    go(x_sum(5))
-    accU[:, quarter(0)] = total_up(quarter(0))
-    accD[:, quarter(0)] = total_dn(quarter(0))
-    for i in (2, 3, 4, 5):
-        x_sum(i).wait_recv()
-
-    def part(a, off, width):
-        cols = pl.ds(pl.multiple_of(x * Q4 + off, 128), width)
-        here = pl.ds(pl.multiple_of(off, 128), width)
-        if a == 0:
-            return accU[:, cols] + rb[3, :, here].astype(F32) + rb[4, :, here].astype(F32)
-        return accD[:, cols] + rb[2, :, here].astype(F32) + rb[5, :, here].astype(F32)
-
-    def y_sum(a):
-        return remote(ys.at[a], yr.at[a], sy.at[a], ry.at[a], to_slice)
-
-    def c_sum(h, a):
-        return remote(cs.at[h, a], cb.at[h, a], sc.at[h, a], rc.at[h, a], to_core)
-
-    @pl.when(jnp.logical_not(home))
-    def _():
-        for a in (0, 1):
-            ys[a] = part(a, 0, Q4).astype(BF16)
-            y_sum(a).start()
-        for a in (0, 1):
-            for h in (0, 1):
-                c_sum(h, a).wait_recv()
-        for a in (0, 1):
-            y_sum(a).wait_send()
-
-    @pl.when(home)
-    def _():
-        for a in (0, 1):
-            y_sum(a).wait_recv()
-            for h in (0, 1):
-                theirs = pl.multiple_of(h * 256 + (1 - core) * 128, 128)
-                mine = pl.multiple_of(h * 256 + core * 128, 128)
-                cs[h, a] = (part(a, theirs, 128) + yr[a, :, pl.ds(theirs, 128)].astype(F32)).astype(BF16)
-                c_sum(h, a).start()
-                cb[h, a] = (part(a, mine, 128) + yr[a, :, pl.ds(mine, 128)].astype(F32)).astype(BF16)
-        for a in (0, 1):
-            for h in (0, 1):
-                c_sum(h, a).wait_send()
         for c in w_send:
             c.wait_send()
 
-    def z_sum(a):
-        return remote(cb.at[1 - zhi, a], zr.at[a], sz.at[a], rz.at[a], to_zhi)
-
-    for a in (0, 1):
-        go(z_sum(a))
     for c in loads[2:]:
         c.wait()
 
@@ -316,7 +347,7 @@
         return o_up.at[at, :] if a == 0 else o_dn.at[:, at]
 
     z_sum(0).wait_recv()
-    mean = (cb[zhi, 0].astype(F32) + zr[0].astype(F32)).T * (inner_rate / replicas)
+    mean = (cb[1, 0].astype(F32) + zr[0].astype(F32)).T * (inner_rate / replicas)
     moment = momentum_factor * muv[...] + mean
     o_mu[...] = moment
     o_up[pl.ds(share_row, 128), :] = (
@@ -331,7 +362,7 @@
 
     go(a_z(0))
     z_sum(1).wait_recv()
-    mean = (cb[zhi, 1].astype(F32) + zr[1].astype(F32)) * (inner_rate / replicas)
+    mean = (cb[1, 1].astype(F32) + zr[1].astype(F32)) * (inner_rate / replicas)
     moment = momentum_factor * mdv[...] + mean
     o_md[...] = moment
     o_dn[:, pl.ds(share_row, 128)] = (
@@ -401,15 +432,15 @@
             jax.ShapeDtypeStruct(up_moment.shape, F32),
             jax.ShapeDtypeStruct(down_moment.shape, F32),
         ),
-        in_specs=[pl.BlockSpec(memory_space=pl.ANY)] * 6,
+        in_specs=[pl.BlockSpec(memory_space=pltpu.HBM)] * 6,
         out_specs=[pl.BlockSpec(memory_space=pltpu.VMEM)] * 4,
         scratch_shapes=[
             vmem((8 * SLAB, D), BF16), vmem((8 * SLAB, D), BF16),
             vmem((D, FL), BF16), vmem((FL, D), BF16),
             vmem((FL, D), F32), vmem((FL, D), F32),
-            vmem((FL, 2 * SLAB), BF16), vmem((FL, 2 * SLAB), BF16),
-            vmem((6, FL, Q4), BF16), vmem((6, FL, Q4), BF16),
-            vmem((2, FL, Q4), BF16), vmem((2, FL, Q4), BF16),
+            vmem((FL, SLAB), BF16), vmem((FL, SLAB), BF16),
+            vmem((2, 6, FL, Q4 // 2), BF16), vmem((2, 6, FL, Q4 // 2), BF16),
+            vmem((2, 2, FL, Q4 // 2), BF16), vmem((2, 2, FL, Q4 // 2), BF16),
             vmem((2, 2, FL, 128), BF16), vmem((2, 2, FL, 128), BF16),
             vmem((2, FL, 128), BF16),
             vmem((128, FL), BF16), vmem((FL, 128), BF16),
@@ -417,11 +448,11 @@
             dma((8,)),
             dma((8,)), dma((8,)), dma((8, 2)), dma((8, 2)), dma((8,)), dma((8,)), dma((1,)), dma((1,)),
             dma((8, 2)), dma((8, 2)), dma((8, 2)), dma((8, 2)), dma((2,)), dma((2,)),
-            dma((6,)), dma((6,)), dma((2,)), dma((2,)), dma((2, 2)), dma((2, 2)), dma((2,)), dma((2,)),
+            dma((2, 6)), dma((2, 6)), dma((2, 2)), dma((2, 2)), dma((2, 2)), dma((2, 2)), dma((2,)), dma((2,)),
             dma((2, 4, 2)), dma((2, 4, 2)), dma((2, 4, 2)), dma((2, 4, 2)),
         ],
         compiler_params=pltpu.CompilerParams(
-            collective_id=0, has_side_effects=True, vmem_limit_bytes=48 << 20
+            collective_id=0, has_side_effects=True, vmem_limit_bytes=60 << 20
         ),
         name="outer_round",
     )(tokens_in[0], cotangent[0], up_weight, down_weight, up_moment, down_moment)

time: 155 us -> 139 us (0.90)
  Pallas kernels: 145 us -> 133 us
  local copies, waits for them, and re-layouts: 9.35 us -> 4.98 us
    pallas_call x1, Pallas kernels: 145 us -> 133 us  [local(): pl.pallas_call(outer_round, out_shape=(jax.ShapeDtypeStruct(up_weight.sha...]
    unnamed x16 -> x10, local copies, waits for them, and re-layouts: 9.35 us -> 4.98 us
where the time goes in v2:
time: 139 us; the launch traced here: 138 us
  Pallas kernels  133 us (96%)
  local copies, waits for them, and re-layouts  4.98 us (4%)
    pallas_call x1, Pallas kernels, local(): pl.pallas_call(outer_round, out_shape=(jax.ShapeDtypeStruct(up_weight.sha...  133 us
    unnamed x10, local copies, waits for them, and re-layouts  4.98 us

profile of v2, /device:TPU:1, one launch (start us, length us, event | category | flops | bytes accessed | tf_op | source)
XLA Modules:
  0.0 138.3 jit_solution(9061503299675736250)
XLA Ops:
  0.6 132.7 %outer_round.1 = (bf16[2048,256]{1,0:T(8,128)(2,1)}, bf16[256,2048]{1,0:T(8,128)(2,1)}, f32[128,256]{1,0:T(8,128)}, f32[256,128]{1,0:T(8,128)}) custom-call(bf16[48,2048]{1,0:T(8,128)(2,1)} %bitcast.2, bf16[48,2048]{1,0:T(8,128)(2,1)} %bitcast.3, bf16[2048,256]{1,0:T(8,128)(2,1)} %up.1, bf16[256,2048]{1,0:T(8,128)(2,1)} %down.1, f32[128,256]{1,0:T(8,128)} %mu.1, ...), custom_call_target="tpu_custom_call" | custom-call | tf_op jit(solution)/shard_map/outer_round/pallas_call | solution.py:427
  133.3 0.0 copy-start
  133.3 2.4 %copy.14 = bf16[2048,256]{1,0:T(8,128)(2,1)} copy(bf16[2048,256]{1,0:T(8,128)(2,1)} %get-tuple-element.8) | data formatting | bytes 2097152
  135.7 0.0 copy-done
  135.7 0.0 copy-start.2
  135.7 1.0 copy.15
  136.7 0.1 copy-done.2
  136.7 0.0 copy-start.1
  136.7 0.7 copy.16
  137.4 0.3 copy-done.1
  137.7 0.7 copy.17
Async XLA Ops:
  133.3 2.4 %copy-start = (bf16[256,2048]{1,0:T(8,128)(2,1)S(1)}, bf16[256,2048]{1,0:T(8,128)(2,1)}, u32[]{:S(2)}) copy-start(bf16[256,2048]{1,0:T(8,128)(2,1)} %get-tuple-element.9) | copy-start | bytes 3145732
  135.7 1.0 copy-start.2
  136.7 1.0 copy-start.1

commit v3 on v2

v3 whole, which is shorter than its diff:
```python
import functools

import jax
import jax.numpy as jnp
from jax import lax
from jax.experimental import pallas as pl
from jax.experimental.pallas import tpu as pltpu
from jax.sharding import PartitionSpec as P

inner_rate = 0.3
outer_rate = 0.7
momentum_factor = 0.9

MESH = pl.DeviceIdType.MESH
F32 = jnp.float32
BF16 = jnp.bfloat16

ROWS = 48
SLAB = 4 * ROWS
D = 2048
FL = 256
Q4 = D // 4


def device(x, zhi, core, zlo, y):
    return {"rep": (x * 2 + zhi) * 2 + core, "fsdp": zlo * 4 + y}


def outer_round(
    tok, cot, up, down, mu, md,
    o_up, o_dn, o_mu, o_md,
    X, G, Wu, Wd, accU, accD, dT, aT, sb, rb, ys, yr, cs, cb, zr, us, ds, muv, mdv, W,
    ld, sxz, rxz, sgz, rgz, sxy, rxy, sgy, rgy, sxc, rxc, sgc, rgc, sw, rw,
    sx, rx, sy, ry, sc, rc, sz, rz, sA, rA, sC, rC,
):
    rep = lax.axis_index("rep")
    fs = lax.axis_index("fsdp")
    x, zhi, core = rep // 4, (rep // 2) % 2, rep % 2
    zlo, y = fs // 4, fs % 4
    z = zhi * 8 + zlo
    sgn = 1 - 2 * core

    def at_z(zz):
        zz = (zz + 32) % 16
        return device(x, zz // 8, core, zz % 8, y)

    def at_x(xx):
        return device((xx + 8) % 4, zhi, core, zlo, y)

    to_long = at_z(z + sgn)
    to_short = at_z(z - sgn)
    to_pair = device(x, zhi, core, zlo, y + 1 - 2 * (y % 2))
    to_slice = device(x, zhi, core, zlo, 3 - y)
    to_core = device(x, zhi, 1 - core, zlo, y)
    to_right = at_x(x + 1)
    to_left = at_x(x - 1)
    to_zhi = device(x, 1 - zhi, core, zlo, y)
    home = (y % 2) == core

    def local(src, dst, sem):
        return pltpu.make_async_copy(src, dst, sem)

    def remote(src, dst, ssem, rsem, to):
        return pltpu.make_async_remote_copy(
            src_ref=src, dst_ref=dst, send_sem=ssem, recv_sem=rsem,
            device_id=to, device_id_type=MESH,
        )

    def slot(buf, zi, yi, ci):
        return buf.at[pl.ds(zi * SLAB + (yi * 2 + ci) * ROWS, ROWS), :]

    share_row = pl.multiple_of(rep * 128, 128)
    loads = [
        local(tok, slot(X, 0, 0, 0), ld.at[0]),
        local(cot, slot(G, 0, 0, 0), ld.at[1]),
        local(up.at[pl.ds(share_row, 128), :], us, ld.at[2]),
        local(down.at[:, pl.ds(share_row, 128)], ds, ld.at[3]),
        local(mu, muv, ld.at[4]),
        local(md, mdv, ld.at[5]),
    ]
    for c in loads:
        c.start()

    barrier = pltpu.get_barrier_semaphore()
    everyone = (to_long, to_short, to_pair, to_slice, to_core, to_right, to_left, to_zhi)
    for other in everyone:
        pl.semaphore_signal(barrier, inc=1, device_id=other, device_id_type=MESH)
    loads[0].wait()
    loads[1].wait()
    pl.semaphore_wait(barrier, len(everyone))

    sent = []

    def go(copy):
        copy.start()
        sent.append(copy)

    def x_z(src_zi, dst_zi, to):
        return remote(slot(X, src_zi, 0, 0), slot(X, dst_zi, 0, 0), sxz.at[dst_zi], rxz.at[dst_zi], to)

    def g_z(src_zi, dst_zi, yi, to):
        return remote(
            slot(G, src_zi, yi, 0), slot(G, dst_zi, yi, 0), sgz.at[dst_zi, yi], rgz.at[dst_zi, yi], to
        )

    def x_y(zi):
        return remote(slot(X, zi, 0, 0), slot(X, zi, 1, 0), sxy.at[zi], rxy.at[zi], to_pair)

    def g_y():
        return remote(slot(G, 0, 0, 0), slot(G, 0, 1, 0), sgy.at[0], rgy.at[0], to_pair)

    def x_c(zi, yi):
        return remote(slot(X, zi, yi, 0), slot(X, zi, yi, 1), sxc.at[zi, yi], rxc.at[zi, yi], to_core)

    def g_c(zi, yi):
        return remote(slot(G, zi, yi, 0), slot(G, zi, yi, 1), sgc.at[zi, yi], rgc.at[zi, yi], to_core)

    go(g_y())
    go(x_z(0, 1, to_long))
    go(x_z(0, 2, to_short))
    go(g_z(0, 1, 0, to_long))
    go(g_z(0, 2, 0, to_short))
    go(x_y(0))
    go(x_c(0, 0))
    go(g_c(0, 0))

    w_send = [
        remote(up, Wu, sw.at[0], rw.at[0], to_slice),
        remote(down, Wd, sw.at[1], rw.at[1], to_slice),
    ]
    w_local = [local(up, Wu, sw.at[2]), local(down, Wd, sw.at[3])]

    @pl.when(home)
    def _():
        for c in w_send + w_local:
            c.start()

    g_y().wait_recv()
    go(g_z(0, 1, 1, to_long))
    go(g_z(0, 2, 1, to_short))
    go(g_c(0, 1))
    x_y(0).wait_recv()
    go(x_c(0, 1))

    def arrived_x(zi, onward, to):
        x_z(0, zi, to_long).wait_recv()
        if onward:
            go(x_z(zi, zi + 2, to))
        go(x_y(zi))
        go(x_c(zi, 0))

    def arrived_g(zi, yi, onward, to):
        g_z(0, zi, yi, to_long).wait_recv()
        if onward:
            go(g_z(zi, zi + 2, yi, to))
        go(g_c(zi, yi))

    def arrived_pair(zi):
        x_y(zi).wait_recv()
        go(x_c(zi, 1))

    def from_core(zi):
        for yi in (0, 1):
            x_c(zi, yi).wait_recv()
            g_c(zi, yi).wait_recv()

    def middle(zi):
        rows = pl.ds(zi * SLAB, SLAB)
        pre = jnp.dot(X[rows, :], Wu[...], preferred_element_type=F32)
        back = lax.dot_general(G[rows, :], Wd[...], (((1,), (1,)), ((), ())), preferred_element_type=F32)
        s = jax.nn.sigmoid(pre)
        act = pre * s
        dpre = back * s * (1.0 + pre * (1.0 - s))
        dT[...] = dpre.astype(BF16).T
        aT[...] = act.astype(BF16).T

    def grads(zi):
        rows = pl.ds(zi * SLAB, SLAB)

        @pl.loop(0, D // 256)
        def _(j):
            cols = pl.ds(pl.multiple_of(j * 256, 256), 256)
            du = jnp.dot(dT[...], X[rows, cols], preferred_element_type=F32)
            dd = jnp.dot(aT[...], G[rows, cols], preferred_element_type=F32)
            accU[:, cols] = du if zi == 0 else accU[:, cols] + du
            accD[:, cols] = dd if zi == 0 else accD[:, cols] + dd

    def unit(zi):
        from_core(zi)
        middle(zi)
        grads(zi)

    for k in (1, 2, 3):
        long, short = 2 * k - 1, 2 * k
        arrived_x(long, True, to_long)
        arrived_x(short, k < 3, to_short)
        if k == 3:
            unit(1)
        arrived_g(long, 0, True, to_long)
        arrived_g(short, 0, k < 3, to_short)
        if k == 3:
            unit(2)
        arrived_pair(long)
        arrived_pair(short)
        if k == 3:
            unit(3)
        arrived_g(long, 1, True, to_long)
        arrived_g(short, 1, k < 3, to_short)
        if k == 2:

            @pl.when(home)
            def _():
                for c in w_local:
                    c.wait()

            @pl.when(jnp.logical_not(home))
            def _():
                for c in w_send:
                    c.wait_recv()

            unit(0)
        if k == 3:
            unit(4)

    arrived_x(7, False, to_long)
    unit(5)
    arrived_g(7, 0, False, to_long)
    unit(6)
    arrived_pair(7)
    arrived_g(7, 1, False, to_long)
    from_core(7)
    middle(7)

    last = pl.ds(7 * SLAB, SLAB)
    H4 = Q4 // 2
    HR = FL // 2
    half = (1 - zhi, zhi)

    def hidden(m):
        return pl.ds(m * HR, HR)

    def cols(step, i):
        return pl.ds(pl.multiple_of(((x + step) % 4) * Q4 + half[i] * H4, H4), H4)

    def total_up(m, at):
        return accU[hidden(m), at] + jnp.dot(dT[hidden(m), :], X[last, at], preferred_element_type=F32)

    def total_dn(m, at):
        return accD[hidden(m), at] + jnp.dot(aT[hidden(m), :], G[last, at], preferred_element_type=F32)

    def x_sum(m, i, n):
        return remote(
            sb.at[m, i, n], rb.at[m, i, n], sx.at[m, i, n], rx.at[m, i, n],
            to_right if n % 2 == 0 else to_left,
        )

    def x_first(m, i):
        sb[m, i, 0] = total_up(m, cols(2, i)).astype(BF16)
        go(x_sum(m, i, 0))
        sb[m, i, 1] = total_dn(m, cols(2, i)).astype(BF16)
        go(x_sum(m, i, 1))
        sb[m, i, 2] = total_dn(m, cols(1, i)).astype(BF16)
        go(x_sum(m, i, 2))
        sb[m, i, 3] = total_up(m, cols(3, i)).astype(BF16)
        go(x_sum(m, i, 3))
        for step in (1, 0):
            accU[hidden(m), cols(step, i)] = total_up(m, cols(step, i))
        for step in (3, 0):
            accD[hidden(m), cols(step, i)] = total_dn(m, cols(step, i))

    def x_relay(m, i):
        x_sum(m, i, 0).wait_recv()
        sb[m, i, 4] = (accU[hidden(m), cols(1, i)] + rb[m, i, 0].astype(F32)).astype(BF16)
        go(x_sum(m, i, 4))
        x_sum(m, i, 1).wait_recv()
        sb[m, i, 5] = (accD[hidden(m), cols(3, i)] + rb[m, i, 1].astype(F32)).astype(BF16)
        go(x_sum(m, i, 5))

    def part(m, i, a, off, width):
        at = pl.ds(pl.multiple_of(x * Q4 + half[i] * H4 + off, 128), width)
        here = pl.ds(pl.multiple_of(off, 128), width)
        if a == 0:
            return accU[hidden(m), at] + rb[m, i, 3, :, here].astype(F32) + rb[m, i, 4, :, here].astype(F32)
        return accD[hidden(m), at] + rb[m, i, 2, :, here].astype(F32) + rb[m, i, 5, :, here].astype(F32)

    def y_sum(m, i):
        return remote(ys.at[m, i], yr.at[m, i], sy.at[m, i], ry.at[m, i], to_slice)

    def c_sum(m, i):
        return remote(cs.at[m, i], cb.at[m, i], sc.at[m, i], rc.at[m, i], to_core)

    def y_out(m, i):
        for n in (2, 3, 4, 5):
            x_sum(m, i, n).wait_recv()

        @pl.when(jnp.logical_not(home))
        def _():
            for a in (0, 1):
                ys[m, i, a] = part(m, i, a, 0, H4).astype(BF16)
            y_sum(m, i).start()

    def y_in(m, i):
        @pl.when(jnp.logical_not(home))
        def _():
            c_sum(m, i).wait_recv()

        @pl.when(home)
        def _():
            y_sum(m, i).wait_recv()
            theirs = pl.multiple_of((1 - core) * 128, 128)
            mine = pl.multiple_of(core * 128, 128)
            for a in (0, 1):
                cs[m, i, a] = (
                    part(m, i, a, theirs, 128) + yr[m, i, a, :, pl.ds(theirs, 128)].astype(F32)
                ).astype(BF16)
            c_sum(m, i).start()
            for a in (0, 1):
                cb[m, i, a] = (
                    part(m, i, a, mine, 128) + yr[m, i, a, :, pl.ds(mine, 128)].astype(F32)
                ).astype(BF16)

    def z_sum(m):
        return remote(cb.at[m, 0], zr.at[m], sz.at[m], rz.at[m], to_zhi)

    def outer_step(m):
        scale = inner_rate / 16
        z_sum(m).wait_recv()
        mean = (cb[m, 1, 0].astype(F32) + zr[m, 0].astype(F32)).T * scale
        moment = momentum_factor * muv[:, hidden(m)] + mean
        o_mu[:, hidden(m)] = moment
        W[rep, m, 0] = (
            us[:, hidden(m)].astype(F32) - outer_rate * (mean + momentum_factor * moment)
        ).astype(BF16)
        mean = (cb[m, 1, 1].astype(F32) + zr[m, 1].astype(F32)) * scale
        moment = momentum_factor * mdv[hidden(m), :] + mean
        o_md[hidden(m), :] = moment
        W[rep, m, 1] = (
            ds[hidden(m), :].astype(F32) - outer_rate * (mean + momentum_factor * moment)
        ).astype(BF16)
        go(a_z(m))
        x_out(0, m)

    back_by = {0: 0, 1: 1, 2: 2, 3: -1}

    def share(q, j, cc):
        return (((x - back_by[j] + 4) % 4) * 2 + (zhi + q) % 2) * 2 + cc

    def a_z(m):
        block = W.at[rep, m]
        return remote(block, block, sA.at[1, 0, m, 0], rA.at[1, 0, m, 0], to_zhi)

    def z_in(m):
        block = W.at[share(1, 0, core), m]
        return remote(block, block, sA.at[1, 0, m, 0], rA.at[1, 0, m, 0], to_zhi)

    def a_x(a, m, q, j, dst_j, to):
        block = W.at[share(q, j, core), m, a]
        return remote(block, block, sA.at[q, dst_j, m, a], rA.at[q, dst_j, m, a], to)

    def x_in(a, m, q, j):
        block = W.at[share(q, j, core), m, a]
        return remote(block, block, sA.at[q, j, m, a], rA.at[q, j, m, a], to_right)

    def a_c(m, q, j):
        block = W.at[share(q, j, core), m]
        return remote(block, block, sC.at[q, j, m], rC.at[q, j, m], to_core)

    def c_in(m, q, j):
        block = W.at[share(q, j, 1 - core), m]
        return remote(block, block, sC.at[q, j, m], rC.at[q, j, m], to_core)

    def place(m, q, j, cc):
        r = share(q, j, cc)
        at = pl.ds(pl.multiple_of(r * 128, 128), 128)
        o_up[at, hidden(m)] = W[r, m, 0]
        o_dn[hidden(m), at] = W[r, m, 1]

    def x_out(q, m):
        if q == 1:
            z_in(m).wait_recv()
        go(a_x(0, m, q, 0, 1, to_right))
        go(a_x(1, m, q, 0, 3, to_left))
        go(a_x(1, m, q, 0, 1, to_right))
        go(a_x(0, m, q, 0, 3, to_left))
        go(a_c(m, q, 0))

    def x_pass(q, m):
        x_in(0, m, q, 1).wait_recv()
        go(a_x(0, m, q, 1, 2, to_right))
        x_in(1, m, q, 3).wait_recv()
        go(a_x(1, m, q, 3, 2, to_left))
        x_in(1, m, q, 1).wait_recv()
        go(a_c(m, q, 1))
        x_in(0, m, q, 3).wait_recv()
        go(a_c(m, q, 3))
        place(m, q, 0, core)
        place(m, q, 1, core)
        place(m, q, 3, core)
        for a in (0, 1):
            x_in(a, m, q, 2).wait_recv()
        go(a_c(m, q, 2))
        place(m, q, 2, core)

    def from_other(q, m):
        for j in (0, 1, 3, 2):
            c_in(m, q, j).wait_recv()
            place(m, q, j, 1 - core)

    def settle(copies):
        for c in copies:
            c.wait_send()

    x_first(0, 0)
    x_relay(0, 0)
    x_first(1, 0)
    y_out(0, 0)
    x_relay(1, 0)
    x_first(0, 1)
    y_in(0, 0)
    go(z_sum(0))
    y_out(1, 0)
    x_relay(0, 1)
    x_first(1, 1)
    y_in(1, 0)
    go(z_sum(1))
    y_out(0, 1)
    x_relay(1, 1)
    y_in(0, 1)
    y_out(1, 1)
    for c in loads[2:]:
        c.wait()
    early = list(sent)
    sent.clear()
    outer_step(0)
    y_in(1, 1)
    x_pass(0, 0)

    outer_step(1)
    settle(early)

    @pl.when(home)
    def _():
        for c in w_send:
            c.wait_send()
        for m in (0, 1):
            for i in (0, 1):
                c_sum(m, i).wait_send()

    @pl.when(jnp.logical_not(home))
    def _():
        for m in (0, 1):
            for i in (0, 1):
                y_sum(m, i).wait_send()

    from_other(0, 0)
    x_out(1, 0)
    x_pass(0, 1)
    x_pass(1, 0)
    from_other(0, 1)
    x_out(1, 1)
    from_other(1, 0)
    x_pass(1, 1)
    from_other(1, 1)
    settle(sent)


def local(tokens_in, cotangent, up_weight, down_weight, up_moment, down_moment):
    dma = pltpu.SemaphoreType.DMA
    vmem = pltpu.VMEM
    return pl.pallas_call(
        outer_round,
        out_shape=(
            jax.ShapeDtypeStruct(up_weight.shape, BF16),
            jax.ShapeDtypeStruct(down_weight.shape, BF16),
            jax.ShapeDtypeStruct(up_moment.shape, F32),
            jax.ShapeDtypeStruct(down_moment.shape, F32),
        ),
        in_specs=[pl.BlockSpec(memory_space=pltpu.HBM)] * 6,
        out_specs=[pl.BlockSpec(memory_space=pltpu.VMEM)] * 4,
        scratch_shapes=[
            vmem((8 * SLAB, D), BF16), vmem((8 * SLAB, D), BF16),
            vmem((D, FL), BF16), vmem((FL, D), BF16),
            vmem((FL, D), F32), vmem((FL, D), F32),
            vmem((FL, SLAB), BF16), vmem((FL, SLAB), BF16),
            vmem((2, 2, 6, FL // 2, Q4 // 2), BF16), vmem((2, 2, 6, FL // 2, Q4 // 2), BF16),
            vmem((2, 2, 2, FL // 2, Q4 // 2), BF16), vmem((2, 2, 2, FL // 2, Q4 // 2), BF16),
            vmem((2, 2, 2, FL // 2, 128), BF16), vmem((2, 2, 2, FL // 2, 128), BF16),
            vmem((2, 2, FL // 2, 128), BF16),
            vmem((128, FL), BF16), vmem((FL, 128), BF16),
            vmem((128, FL), F32), vmem((FL, 128), F32),
            vmem((16, 2, 2, FL // 2, 128), BF16),
            dma((6,)),
            dma((8,)), dma((8,)), dma((8, 2)), dma((8, 2)), dma((8,)), dma((8,)), dma((1,)), dma((1,)),
            dma((8, 2)), dma((8, 2)), dma((8, 2)), dma((8, 2)), dma((4,)), dma((2,)),
            dma((2, 2, 6)), dma((2, 2, 6)), dma((2, 2)), dma((2, 2)), dma((2, 2)), dma((2, 2)), dma((2,)), dma((2,)),
            dma((2, 4, 2, 2)), dma((2, 4, 2, 2)), dma((2, 4, 2)), dma((2, 4, 2)),
        ],
        compiler_params=pltpu.CompilerParams(
            collective_id=0, has_side_effects=True, vmem_limit_bytes=60 << 20
        ),
        name="outer_round",
    )(tokens_in[0], cotangent[0], up_weight, down_weight, up_moment, down_moment)


def solution(mesh):
    return jax.shard_map(
        local,
        mesh=mesh,
        in_specs=(
            P("rep", "fsdp", None),
            P("rep", "fsdp", None),
            P(None, "fsdp"),
            P("fsdp", None),
            P("rep", "fsdp"),
            P("fsdp", "rep"),
        ),
        out_specs=(P(None, "fsdp"), P("fsdp", None), P("rep", "fsdp"), P("fsdp", "rep")),
        check_vma=False,
    )
```

time: 139 us -> 131 us (0.942)
  Pallas kernels: 133 us -> 126 us
    pallas_call x1, Pallas kernels: 133 us -> 126 us  [local(): pl.pallas_call(outer_round, out_shape=(jax.ShapeDtypeStruct(up_weight.sha...]
where the time goes in v3:
time: 131 us
  Pallas kernels  126 us (96%)
  local copies, waits for them, and re-layouts  4.98 us (4%)
    pallas_call x1, Pallas kernels, local(): pl.pallas_call(outer_round, out_shape=(jax.ShapeDtypeStruct(up_weight.sha...  126 us
    unnamed x10, local copies, waits for them, and re-layouts  4.98 us

profile of v3, /device:TPU:1, one launch (start us, length us, event | category | flops | bytes accessed | tf_op | source)
XLA Modules:
  0.0 131.1 jit_solution(17025837602198416676)
XLA Ops:
  0.6 125.5 %outer_round.1 = (bf16[2048,256]{1,0:T(8,128)(2,1)}, bf16[256,2048]{1,0:T(8,128)(2,1)}, f32[128,256]{1,0:T(8,128)}, f32[256,128]{1,0:T(8,128)}) custom-call(bf16[48,2048]{1,0:T(8,128)(2,1)} %bitcast.2, bf16[48,2048]{1,0:T(8,128)(2,1)} %bitcast.3, bf16[2048,256]{1,0:T(8,128)(2,1)} %up.1, bf16[256,2048]{1,0:T(8,128)(2,1)} %down.1, f32[128,256]{1,0:T(8,128)} %mu.1, ...), custom_call_target="tpu_custom_call" | custom-call | tf_op jit(solution)/shard_map/outer_round/pallas_call | solution.py:470
  126.2 0.0 copy-start
  126.2 2.4 %copy.14 = bf16[2048,256]{1,0:T(8,128)(2,1)} copy(bf16[2048,256]{1,0:T(8,128)(2,1)} %get-tuple-element.8) | data formatting | bytes 2097152
  128.5 0.0 copy-done
  128.5 0.0 copy-start.2
  128.5 1.0 copy.15
  129.5 0.1 copy-done.2
  129.5 0.0 copy-start.1
  129.5 0.7 copy.16
  130.2 0.3 copy-done.1
  130.5 0.7 copy.17
Async XLA Ops:
  126.2 2.4 %copy-start = (bf16[256,2048]{1,0:T(8,128)(2,1)S(1)}, bf16[256,2048]{1,0:T(8,128)(2,1)}, u32[]{:S(2)}) copy-start(bf16[256,2048]{1,0:T(8,128)(2,1)} %get-tuple-element.9) | copy-start | bytes 3145732
  128.5 1.0 copy-start.2
  129.5 1.0 copy-start.1

commit v4 on v3

--- a/solution.py
+++ b/solution.py
@@ -29,9 +29,9 @@
 def outer_round(
     tok, cot, up, down, mu, md,
     o_up, o_dn, o_mu, o_md,
-    X, G, Wu, Wd, accU, accD, dT, aT, sb, rb, ys, yr, cs, cb, zr, us, ds, muv, mdv, W,
+    X, G, Wu, Wd, accU, accD, dT, aT, sb, rb, ys, yr, cs, cr, cb, zr, us, ds, muv, mdv, W,
     ld, sxz, rxz, sgz, rgz, sxy, rxy, sgy, rgy, sxc, rxc, sgc, rgc, sw, rw,
-    sx, rx, sy, ry, sc, rc, sz, rz, sA, rA, sC, rC,
+    sx, rx, sy, ry, sc, rc, sz, rz, sA, rA, sC, rC, notes,
 ):
     rep = lax.axis_index("rep")
     fs = lax.axis_index("fsdp")
@@ -52,6 +52,8 @@
     to_pair = device(x, zhi, core, zlo, y + 1 - 2 * (y % 2))
     to_slice = device(x, zhi, core, zlo, 3 - y)
     to_core = device(x, zhi, 1 - core, zlo, y)
+    to_cross = device(x, zhi, 1 - core, zlo, 3 - y)
+    to_across = at_x(x + 2)
     to_right = at_x(x + 1)
     to_left = at_x(x - 1)
     to_zhi = device(x, 1 - zhi, core, zlo, y)
@@ -82,12 +84,22 @@
         c.start()
 
     barrier = pltpu.get_barrier_semaphore()
-    everyone = (to_long, to_short, to_pair, to_slice, to_core, to_right, to_left, to_zhi)
+    everyone = (
+        to_long, to_short, to_pair, to_slice, to_core, to_cross, to_right, to_left, to_across,
+    )
     for other in everyone:
         pl.semaphore_signal(barrier, inc=1, device_id=other, device_id_type=MESH)
     loads[0].wait()
     loads[1].wait()
     pl.semaphore_wait(barrier, len(everyone))
+
+    def pass_note(k):
+        if k > 0:
+            pl.semaphore_wait(notes.at[k - 1], 1)
+        if k < 7:
+            pl.semaphore_signal(notes.at[k], inc=1, device_id=to_long, device_id_type=MESH)
+
+    pass_note(0)
 
     sent = []
 
@@ -135,12 +147,14 @@
         for c in w_send + w_local:
             c.start()
 
+    pass_note(1)
     g_y().wait_recv()
     go(g_z(0, 1, 1, to_long))
     go(g_z(0, 2, 1, to_short))
     go(g_c(0, 1))
     x_y(0).wait_recv()
     go(x_c(0, 1))
+    pass_note(2)
 
     def arrived_x(zi, onward, to):
         x_z(0, zi, to_long).wait_recv()
@@ -194,6 +208,8 @@
         long, short = 2 * k - 1, 2 * k
         arrived_x(long, True, to_long)
         arrived_x(short, k < 3, to_short)
+        if k < 3:
+            pass_note(2 * k + 1)
         if k == 3:
             unit(1)
         arrived_g(long, 0, True, to_long)
@@ -206,6 +222,10 @@
             unit(3)
         arrived_g(long, 1, True, to_long)
         arrived_g(short, 1, k < 3, to_short)
+        if k < 3:
+            pass_note(2 * k + 2)
+        else:
+            pass_note(7)
         if k == 2:
 
             @pl.when(home)
@@ -283,11 +303,17 @@
             return accU[hidden(m), at] + rb[m, i, 3, :, here].astype(F32) + rb[m, i, 4, :, here].astype(F32)
         return accD[hidden(m), at] + rb[m, i, 2, :, here].astype(F32) + rb[m, i, 5, :, here].astype(F32)
 
-    def y_sum(m, i):
-        return remote(ys.at[m, i], yr.at[m, i], sy.at[m, i], ry.at[m, i], to_slice)
+    def y_home(m, i):
+        return remote(ys.at[m, i, 0], yr.at[m, i], sy.at[m, i, 0], ry.at[m, i], to_slice)
+
+    def y_cross(m, i):
+        return remote(ys.at[m, i, 1], yr.at[m, i], sy.at[m, i, 1], ry.at[m, i], to_cross)
 
     def c_sum(m, i):
-        return remote(cs.at[m, i], cb.at[m, i], sc.at[m, i], rc.at[m, i], to_core)
+        return remote(cs.at[m, i], cr.at[m, i], sc.at[m, i], rc.at[m, i], to_core)
+
+    mine = pl.multiple_of(core * 128, 128)
+    theirs = pl.multiple_of((1 - core) * 128, 128)
 
     def y_out(m, i):
         for n in (2, 3, 4, 5):
@@ -296,28 +322,31 @@
         @pl.when(jnp.logical_not(home))
         def _():
             for a in (0, 1):
-                ys[m, i, a] = part(m, i, a, 0, H4).astype(BF16)
-            y_sum(m, i).start()
+                ys[m, i, 0, a] = part(m, i, a, mine, 128).astype(BF16)
+            y_home(m, i).start()
+            for a in (0, 1):
+                ys[m, i, 1, a] = part(m, i, a, theirs, 128).astype(BF16)
+            y_cross(m, i).start()
+
+        @pl.when(home)
+        def _():
+            for a in (0, 1):
+                cs[m, i, a] = part(m, i, a, theirs, 128).astype(BF16)
+            c_sum(m, i).start()
 
     def y_in(m, i):
         @pl.when(jnp.logical_not(home))
         def _():
             c_sum(m, i).wait_recv()
+            y_cross(m, i).wait_recv()
+            for a in (0, 1):
+                cb[m, i, a] = (cr[m, i, a].astype(F32) + yr[m, i, a].astype(F32)).astype(BF16)
 
         @pl.when(home)
         def _():
-            y_sum(m, i).wait_recv()
-            theirs = pl.multiple_of((1 - core) * 128, 128)
-            mine = pl.multiple_of(core * 128, 128)
+            y_home(m, i).wait_recv()
             for a in (0, 1):
-                cs[m, i, a] = (
-                    part(m, i, a, theirs, 128) + yr[m, i, a, :, pl.ds(theirs, 128)].astype(F32)
-                ).astype(BF16)
-            c_sum(m, i).start()
-            for a in (0, 1):
-                cb[m, i, a] = (
-                    part(m, i, a, mine, 128) + yr[m, i, a, :, pl.ds(mine, 128)].astype(F32)
-                ).astype(BF16)
+                cb[m, i, a] = (part(m, i, a, mine, 128) + yr[m, i, a].astype(F32)).astype(BF16)
 
     def z_sum(m):
         return remote(cb.at[m, 0], zr.at[m], sz.at[m], rz.at[m], to_zhi)
@@ -347,19 +376,19 @@
 
     def a_z(m):
         block = W.at[rep, m]
-        return remote(block, block, sA.at[1, 0, m, 0], rA.at[1, 0, m, 0], to_zhi)
+        return remote(block, block, sA.at[1, 0, m], rA.at[1, 0, m], to_zhi)
 
     def z_in(m):
         block = W.at[share(1, 0, core), m]
-        return remote(block, block, sA.at[1, 0, m, 0], rA.at[1, 0, m, 0], to_zhi)
-
-    def a_x(a, m, q, j, dst_j, to):
-        block = W.at[share(q, j, core), m, a]
-        return remote(block, block, sA.at[q, dst_j, m, a], rA.at[q, dst_j, m, a], to)
-
-    def x_in(a, m, q, j):
-        block = W.at[share(q, j, core), m, a]
-        return remote(block, block, sA.at[q, j, m, a], rA.at[q, j, m, a], to_right)
+        return remote(block, block, sA.at[1, 0, m], rA.at[1, 0, m], to_zhi)
+
+    def a_x(m, q, dst_j, to):
+        block = W.at[share(q, 0, core), m]
+        return remote(block, block, sA.at[q, dst_j, m], rA.at[q, dst_j, m], to)
+
+    def x_in(m, q, j):
+        block = W.at[share(q, j, core), m]
+        return remote(block, block, sA.at[q, j, m], rA.at[q, j, m], to_right)
 
     def a_c(m, q, j):
         block = W.at[share(q, j, core), m]
@@ -378,28 +407,17 @@
     def x_out(q, m):
         if q == 1:
             z_in(m).wait_recv()
-        go(a_x(0, m, q, 0, 1, to_right))
-        go(a_x(1, m, q, 0, 3, to_left))
-        go(a_x(1, m, q, 0, 1, to_right))
-        go(a_x(0, m, q, 0, 3, to_left))
+        go(a_x(m, q, 2, to_across))
+        go(a_x(m, q, 1, to_right))
+        go(a_x(m, q, 3, to_left))
         go(a_c(m, q, 0))
 
     def x_pass(q, m):
-        x_in(0, m, q, 1).wait_recv()
-        go(a_x(0, m, q, 1, 2, to_right))
-        x_in(1, m, q, 3).wait_recv()
-        go(a_x(1, m, q, 3, 2, to_left))
-        x_in(1, m, q, 1).wait_recv()
-        go(a_c(m, q, 1))
-        x_in(0, m, q, 3).wait_recv()
-        go(a_c(m, q, 3))
         place(m, q, 0, core)
-        place(m, q, 1, core)
-        place(m, q, 3, core)
-        for a in (0, 1):
-            x_in(a, m, q, 2).wait_recv()
-        go(a_c(m, q, 2))
-        place(m, q, 2, core)
+        for j in (1, 3, 2):
+            x_in(m, q, j).wait_recv()
+            go(a_c(m, q, j))
+            place(m, q, j, core)
 
     def from_other(q, m):
         for j in (0, 1, 3, 2):
@@ -450,7 +468,8 @@
     def _():
         for m in (0, 1):
             for i in (0, 1):
-                y_sum(m, i).wait_send()
+                y_home(m, i).wait_send()
+                y_cross(m, i).wait_send()
 
     from_other(0, 0)
     x_out(1, 0)
@@ -483,8 +502,9 @@
             vmem((FL, D), F32), vmem((FL, D), F32),
             vmem((FL, SLAB), BF16), vmem((FL, SLAB), BF16),
             vmem((2, 2, 6, FL // 2, Q4 // 2), BF16), vmem((2, 2, 6, FL // 2, Q4 // 2), BF16),
-            vmem((2, 2, 2, FL // 2, Q4 // 2), BF16), vmem((2, 2, 2, FL // 2, Q4 // 2), BF16),
+            vmem((2, 2, 2, 2, FL // 2, 128), BF16), vmem((2, 2, 2, FL // 2, 128), BF16),
             vmem((2, 2, 2, FL // 2, 128), BF16), vmem((2, 2, 2, FL // 2, 128), BF16),
+            vmem((2, 2, 2, FL // 2, 128), BF16),
             vmem((2, 2, FL // 2, 128), BF16),
             vmem((128, FL), BF16), vmem((FL, 128), BF16),
             vmem((128, FL), F32), vmem((FL, 128), F32),
@@ -492,8 +512,9 @@
             dma((6,)),
             dma((8,)), dma((8,)), dma((8, 2)), dma((8, 2)), dma((8,)), dma((8,)), dma((1,)), dma((1,)),
             dma((8, 2)), dma((8, 2)), dma((8, 2)), dma((8, 2)), dma((4,)), dma((2,)),
-            dma((2, 2, 6)), dma((2, 2, 6)), dma((2, 2)), dma((2, 2)), dma((2, 2)), dma((2, 2)), dma((2,)), dma((2,)),
-            dma((2, 4, 2, 2)), dma((2, 4, 2, 2)), dma((2, 4, 2)), dma((2, 4, 2)),
+            dma((2, 2, 6)), dma((2, 2, 6)), dma((2, 2, 2)), dma((2, 2)), dma((2, 2)), dma((2, 2)), dma((2,)), dma((2,)),
+            dma((2, 4, 2)), dma((2, 4, 2)), dma((2, 4, 2)), dma((2, 4, 2)),
+            pltpu.SemaphoreType.REGULAR((7,)),
         ],
         compiler_params=pltpu.CompilerParams(
             collective_id=0, has_side_effects=True, vmem_limit_bytes=60 << 20

time: 131 us -> 125 us (0.954); the launches traced: 131 us -> 124 us
  Pallas kernels: 126 us -> 118 us
    pallas_call x1, Pallas kernels: 126 us -> 118 us  [local(): pl.pallas_call(outer_round, out_shape=(jax.ShapeDtypeStruct(up_weight.sha...]
where the time goes in v4:
time: 125 us; the launch traced here: 124 us
  Pallas kernels  118 us (94%)
  local copies, waits for them, and re-layouts  4.98 us (4%)
    pallas_call x1, Pallas kernels, local(): pl.pallas_call(outer_round, out_shape=(jax.ShapeDtypeStruct(up_weight.sha...  118 us
    unnamed x10, local copies, waits for them, and re-layouts  4.98 us

profile of v4, /device:TPU:1, one launch (start us, length us, event | category | flops | bytes accessed | tf_op | source)
XLA Modules:
  0.0 123.8 jit_solution(6962824037802061409)
XLA Ops:
  0.6 118.1 %outer_round.1 = (bf16[2048,256]{1,0:T(8,128)(2,1)}, bf16[256,2048]{1,0:T(8,128)(2,1)}, f32[128,256]{1,0:T(8,128)}, f32[256,128]{1,0:T(8,128)}) custom-call(bf16[48,2048]{1,0:T(8,128)(2,1)} %bitcast.2, bf16[48,2048]{1,0:T(8,128)(2,1)} %bitcast.3, bf16[2048,256]{1,0:T(8,128)(2,1)} %up.1, bf16[256,2048]{1,0:T(8,128)(2,1)} %down.1, f32[128,256]{1,0:T(8,128)} %mu.1, ...), custom_call_target="tpu_custom_call" | custom-call | tf_op jit(solution)/shard_map/outer_round/pallas_call | solution.py:489
  118.8 0.0 copy-start
  118.8 2.4 %copy.14 = bf16[2048,256]{1,0:T(8,128)(2,1)} copy(bf16[2048,256]{1,0:T(8,128)(2,1)} %get-tuple-element.8) | data formatting | bytes 2097152
  121.1 0.0 copy-done
  121.1 0.0 copy-start.2
  121.1 1.0 copy.15
  122.1 0.1 copy-done.2
  122.2 0.0 copy-start.1
  122.2 0.7 copy.16
  122.8 0.3 copy-done.1
  123.1 0.7 copy.17
Async XLA Ops:
  118.8 2.4 %copy-start = (bf16[256,2048]{1,0:T(8,128)(2,1)S(1)}, bf16[256,2048]{1,0:T(8,128)(2,1)}, u32[]{:S(2)}) copy-start(bf16[256,2048]{1,0:T(8,128)(2,1)} %get-tuple-element.9) | copy-start | bytes 3145732
  121.1 1.0 copy-start.2
  122.2 1.0 copy-start.1

commit v5 on v4

--- a/solution.py
+++ b/solution.py
@@ -31,7 +31,7 @@
     o_up, o_dn, o_mu, o_md,
     X, G, Wu, Wd, accU, accD, dT, aT, sb, rb, ys, yr, cs, cr, cb, zr, us, ds, muv, mdv, W,
     ld, sxz, rxz, sgz, rgz, sxy, rxy, sgy, rgy, sxc, rxc, sgc, rgc, sw, rw,
-    sx, rx, sy, ry, sc, rc, sz, rz, sA, rA, sC, rC, notes,
+    sx, rx, sy, ry, sc, rc, sz, rz, sA, rA, sC, rC, sw2, rw2, notes,
 ):
     rep = lax.axis_index("rep")
     fs = lax.axis_index("fsdp")
@@ -118,8 +118,8 @@
     def x_y(zi):
         return remote(slot(X, zi, 0, 0), slot(X, zi, 1, 0), sxy.at[zi], rxy.at[zi], to_pair)
 
-    def g_y():
-        return remote(slot(G, 0, 0, 0), slot(G, 0, 1, 0), sgy.at[0], rgy.at[0], to_pair)
+    def g_y(zi):
+        return remote(slot(G, zi, 0, 0), slot(G, zi, 1, 0), sgy.at[zi], rgy.at[zi], to_pair)
 
     def x_c(zi, yi):
         return remote(slot(X, zi, yi, 0), slot(X, zi, yi, 1), sxc.at[zi, yi], rxc.at[zi, yi], to_core)
@@ -127,7 +127,7 @@
     def g_c(zi, yi):
         return remote(slot(G, zi, yi, 0), slot(G, zi, yi, 1), sgc.at[zi, yi], rgc.at[zi, yi], to_core)
 
-    go(g_y())
+    go(g_y(0))
     go(x_z(0, 1, to_long))
     go(x_z(0, 2, to_short))
     go(g_z(0, 1, 0, to_long))
@@ -148,8 +148,7 @@
             c.start()
 
     pass_note(1)
-    g_y().wait_recv()
-    go(g_z(0, 1, 1, to_long))
+    g_y(0).wait_recv()
     go(g_z(0, 2, 1, to_short))
     go(g_c(0, 1))
     x_y(0).wait_recv()
@@ -160,13 +159,17 @@
         x_z(0, zi, to_long).wait_recv()
         if onward:
             go(x_z(zi, zi + 2, to))
-        go(x_y(zi))
+        if zi != 2:
+            go(x_y(zi))
         go(x_c(zi, 0))
 
     def arrived_g(zi, yi, onward, to):
         g_z(0, zi, yi, to_long).wait_recv()
         if onward:
             go(g_z(zi, zi + 2, yi, to))
+        if zi == 1:
+            go(g_y(1))
+            go(x_y(2))
         go(g_c(zi, yi))
 
     def arrived_pair(zi):
@@ -208,6 +211,10 @@
         long, short = 2 * k - 1, 2 * k
         arrived_x(long, True, to_long)
         arrived_x(short, k < 3, to_short)
+        if k == 2:
+            g_y(1).wait_recv()
+            go(g_z(1, 3, 1, to_long))
+            go(g_c(1, 1))
         if k < 3:
             pass_note(2 * k + 1)
         if k == 3:
@@ -220,7 +227,8 @@
         arrived_pair(short)
         if k == 3:
             unit(3)
-        arrived_g(long, 1, True, to_long)
+        if k > 1:
+            arrived_g(long, 1, True, to_long)
         arrived_g(short, 1, k < 3, to_short)
         if k < 3:
             pass_note(2 * k + 2)
@@ -351,6 +359,8 @@
     def z_sum(m):
         return remote(cb.at[m, 0], zr.at[m], sz.at[m], rz.at[m], to_zhi)
 
+    last_z = []
+
     def outer_step(m):
         scale = inner_rate / 16
         z_sum(m).wait_recv()
@@ -360,13 +370,16 @@
         W[rep, m, 0] = (
             us[:, hidden(m)].astype(F32) - outer_rate * (mean + momentum_factor * moment)
         ).astype(BF16)
+        last_z.append(a_z(0, m))
+        last_z[-1].start()
         mean = (cb[m, 1, 1].astype(F32) + zr[m, 1].astype(F32)) * scale
         moment = momentum_factor * mdv[hidden(m), :] + mean
         o_md[hidden(m), :] = moment
         W[rep, m, 1] = (
             ds[hidden(m), :].astype(F32) - outer_rate * (mean + momentum_factor * moment)
         ).astype(BF16)
-        go(a_z(m))
+        last_z.append(a_z(1, m))
+        last_z[-1].start()
         x_out(0, m)
 
     back_by = {0: 0, 1: 1, 2: 2, 3: -1}
@@ -374,13 +387,13 @@
     def share(q, j, cc):
         return (((x - back_by[j] + 4) % 4) * 2 + (zhi + q) % 2) * 2 + cc
 
-    def a_z(m):
-        block = W.at[rep, m]
-        return remote(block, block, sA.at[1, 0, m], rA.at[1, 0, m], to_zhi)
-
-    def z_in(m):
-        block = W.at[share(1, 0, core), m]
-        return remote(block, block, sA.at[1, 0, m], rA.at[1, 0, m], to_zhi)
+    def a_z(a, m):
+        block = W.at[rep, m, a]
+        return remote(block, block, sw2.at[m, a], rw2.at[m, a], to_zhi)
+
+    def z_in(a, m):
+        block = W.at[share(1, 0, core), m, a]
+        return remote(block, block, sw2.at[m, a], rw2.at[m, a], to_zhi)
 
     def a_x(m, q, dst_j, to):
         block = W.at[share(q, 0, core), m]
@@ -406,7 +419,8 @@
 
     def x_out(q, m):
         if q == 1:
-            z_in(m).wait_recv()
+            z_in(0, m).wait_recv()
+            z_in(1, m).wait_recv()
         go(a_x(m, q, 2, to_across))
         go(a_x(m, q, 1, to_right))
         go(a_x(m, q, 3, to_left))
@@ -476,11 +490,13 @@
     x_pass(0, 1)
     x_pass(1, 0)
     from_other(0, 1)
+    settle(sent)
+    sent.clear()
     x_out(1, 1)
     from_other(1, 0)
     x_pass(1, 1)
     from_other(1, 1)
-    settle(sent)
+    settle(sent + last_z)
 
 
 def local(tokens_in, cotangent, up_weight, down_weight, up_moment, down_moment):
@@ -510,11 +526,11 @@
             vmem((128, FL), F32), vmem((FL, 128), F32),
             vmem((16, 2, 2, FL // 2, 128), BF16),
             dma((6,)),
-            dma((8,)), dma((8,)), dma((8, 2)), dma((8, 2)), dma((8,)), dma((8,)), dma((1,)), dma((1,)),
+            dma((8,)), dma((8,)), dma((8, 2)), dma((8, 2)), dma((8,)), dma((8,)), dma((2,)), dma((2,)),
             dma((8, 2)), dma((8, 2)), dma((8, 2)), dma((8, 2)), dma((4,)), dma((2,)),
             dma((2, 2, 6)), dma((2, 2, 6)), dma((2, 2, 2)), dma((2, 2)), dma((2, 2)), dma((2, 2)), dma((2,)), dma((2,)),
             dma((2, 4, 2)), dma((2, 4, 2)), dma((2, 4, 2)), dma((2, 4, 2)),
-            pltpu.SemaphoreType.REGULAR((7,)),
+            dma((2, 2)), dma((2, 2)), pltpu.SemaphoreType.REGULAR((7,)),
         ],
         compiler_params=pltpu.CompilerParams(
             collective_id=0, has_side_effects=True, vmem_limit_bytes=60 << 20

time: 125 us -> 128 us (1.024)
  Pallas kernels: 118 us -> 122 us
    pallas_call x1, Pallas kernels: 118 us -> 122 us  [local(): pl.pallas_call(outer_round, out_shape=(jax.ShapeDtypeStruct(up_weight.sha...]
where the time goes in v5:
time: 128 us; the launch traced here: 127 us
  Pallas kernels  122 us (95%)
  local copies, waits for them, and re-layouts  4.98 us (4%)
    pallas_call x1, Pallas kernels, local(): pl.pallas_call(outer_round, out_shape=(jax.ShapeDtypeStruct(up_weight.sha...  122 us
    unnamed x10, local copies, waits for them, and re-layouts  4.98 us

profile of v5, /device:TPU:1, one launch (start us, length us, event | category | flops | bytes accessed | tf_op | source)
XLA Modules:
  0.0 127.3 jit_solution(11661649533648976512)
XLA Ops:
  0.6 121.7 %outer_round.1 = (bf16[2048,256]{1,0:T(8,128)(2,1)}, bf16[256,2048]{1,0:T(8,128)(2,1)}, f32[128,256]{1,0:T(8,128)}, f32[256,128]{1,0:T(8,128)}) custom-call(bf16[48,2048]{1,0:T(8,128)(2,1)} %bitcast.2, bf16[48,2048]{1,0:T(8,128)(2,1)} %bitcast.3, bf16[2048,256]{1,0:T(8,128)(2,1)} %up.1, bf16[256,2048]{1,0:T(8,128)(2,1)} %down.1, f32[128,256]{1,0:T(8,128)} %mu.1, ...), custom_call_target="tpu_custom_call" | custom-call | tf_op jit(solution)/shard_map/outer_round/pallas_call | solution.py:505
  122.3 0.0 copy-start
  122.3 2.4 %copy.14 = bf16[2048,256]{1,0:T(8,128)(2,1)} copy(bf16[2048,256]{1,0:T(8,128)(2,1)} %get-tuple-element.8) | data formatting | bytes 2097152
  124.7 0.0 copy-done
  124.7 0.0 copy-start.2
  124.7 1.0 copy.15
  125.7 0.1 copy-done.2
  125.7 0.0 copy-start.1
  125.7 0.7 copy.16
  126.4 0.3 copy-done.1
  126.7 0.7 copy.17
Async XLA Ops:
  122.3 2.4 %copy-start = (bf16[256,2048]{1,0:T(8,128)(2,1)S(1)}, bf16[256,2048]{1,0:T(8,128)(2,1)}, u32[]{:S(2)}) copy-start(bf16[256,2048]{1,0:T(8,128)(2,1)} %get-tuple-element.9) | copy-start | bytes 3145732
  124.7 1.0 copy-start.2
  125.7 1.0 copy-start.1

commit v6 on v5

--- a/solution.py
+++ b/solution.py
@@ -118,8 +118,8 @@
     def x_y(zi):
         return remote(slot(X, zi, 0, 0), slot(X, zi, 1, 0), sxy.at[zi], rxy.at[zi], to_pair)
 
-    def g_y(zi):
-        return remote(slot(G, zi, 0, 0), slot(G, zi, 1, 0), sgy.at[zi], rgy.at[zi], to_pair)
+    def g_y():
+        return remote(slot(G, 0, 0, 0), slot(G, 0, 1, 0), sgy.at[0], rgy.at[0], to_pair)
 
     def x_c(zi, yi):
         return remote(slot(X, zi, yi, 0), slot(X, zi, yi, 1), sxc.at[zi, yi], rxc.at[zi, yi], to_core)
@@ -127,7 +127,7 @@
     def g_c(zi, yi):
         return remote(slot(G, zi, yi, 0), slot(G, zi, yi, 1), sgc.at[zi, yi], rgc.at[zi, yi], to_core)
 
-    go(g_y(0))
+    go(g_y())
     go(x_z(0, 1, to_long))
     go(x_z(0, 2, to_short))
     go(g_z(0, 1, 0, to_long))
@@ -148,7 +148,8 @@
             c.start()
 
     pass_note(1)
-    g_y(0).wait_recv()
+    g_y().wait_recv()
+    go(g_z(0, 1, 1, to_long))
     go(g_z(0, 2, 1, to_short))
     go(g_c(0, 1))
     x_y(0).wait_recv()
@@ -159,17 +160,13 @@
         x_z(0, zi, to_long).wait_recv()
         if onward:
             go(x_z(zi, zi + 2, to))
-        if zi != 2:
-            go(x_y(zi))
+        go(x_y(zi))
         go(x_c(zi, 0))
 
     def arrived_g(zi, yi, onward, to):
         g_z(0, zi, yi, to_long).wait_recv()
         if onward:
             go(g_z(zi, zi + 2, yi, to))
-        if zi == 1:
-            go(g_y(1))
-            go(x_y(2))
         go(g_c(zi, yi))
 
     def arrived_pair(zi):
@@ -211,10 +208,6 @@
         long, short = 2 * k - 1, 2 * k
         arrived_x(long, True, to_long)
         arrived_x(short, k < 3, to_short)
-        if k == 2:
-            g_y(1).wait_recv()
-            go(g_z(1, 3, 1, to_long))
-            go(g_c(1, 1))
         if k < 3:
             pass_note(2 * k + 1)
         if k == 3:
@@ -227,8 +220,7 @@
         arrived_pair(short)
         if k == 3:
             unit(3)
-        if k > 1:
-            arrived_g(long, 1, True, to_long)
+        arrived_g(long, 1, True, to_long)
         arrived_g(short, 1, k < 3, to_short)
         if k < 3:
             pass_note(2 * k + 2)
@@ -526,7 +518,7 @@
             vmem((128, FL), F32), vmem((FL, 128), F32),
             vmem((16, 2, 2, FL // 2, 128), BF16),
             dma((6,)),
-            dma((8,)), dma((8,)), dma((8, 2)), dma((8, 2)), dma((8,)), dma((8,)), dma((2,)), dma((2,)),
+            dma((8,)), dma((8,)), dma((8, 2)), dma((8, 2)), dma((8,)), dma((8,)), dma((1,)), dma((1,)),
             dma((8, 2)), dma((8, 2)), dma((8, 2)), dma((8, 2)), dma((4,)), dma((2,)),
             dma((2, 2, 6)), dma((2, 2, 6)), dma((2, 2, 2)), dma((2, 2)), dma((2, 2)), dma((2, 2)), dma((2,)), dma((2,)),
             dma((2, 4, 2)), dma((2, 4, 2)), dma((2, 4, 2)), dma((2, 4, 2)),

time: 128 us -> 126 us (0.984); the launches traced: 127 us -> 124 us
  Pallas kernels: 122 us -> 118 us
    pallas_call x1, Pallas kernels: 122 us -> 118 us  [local(): pl.pallas_call(outer_round, out_shape=(jax.ShapeDtypeStruct(up_weight.sha...]
where the time goes in v6:
time: 126 us; the launch traced here: 124 us
  Pallas kernels  118 us (94%)
  local copies, waits for them, and re-layouts  4.98 us (4%)
    pallas_call x1, Pallas kernels, local(): pl.pallas_call(outer_round, out_shape=(jax.ShapeDtypeStruct(up_weight.sha...  118 us
    unnamed x10, local copies, waits for them, and re-layouts  4.98 us

profile of v6, /device:TPU:1, one launch (start us, length us, event | category | flops | bytes accessed | tf_op | source)
XLA Modules:
  0.0 124.0 jit_solution(12703176042145497501)
XLA Ops:
  0.6 118.4 %outer_round.1 = (bf16[2048,256]{1,0:T(8,128)(2,1)}, bf16[256,2048]{1,0:T(8,128)(2,1)}, f32[128,256]{1,0:T(8,128)}, f32[256,128]{1,0:T(8,128)}) custom-call(bf16[48,2048]{1,0:T(8,128)(2,1)} %bitcast.2, bf16[48,2048]{1,0:T(8,128)(2,1)} %bitcast.3, bf16[2048,256]{1,0:T(8,128)(2,1)} %up.1, bf16[256,2048]{1,0:T(8,128)(2,1)} %down.1, f32[128,256]{1,0:T(8,128)} %mu.1, ...), custom_call_target="tpu_custom_call" | custom-call | tf_op jit(solution)/shard_map/outer_round/pallas_call | solution.py:497
  119.0 0.0 copy-start
  119.0 2.4 %copy.14 = bf16[2048,256]{1,0:T(8,128)(2,1)} copy(bf16[2048,256]{1,0:T(8,128)(2,1)} %get-tuple-element.8) | data formatting | bytes 2097152
  121.4 0.0 copy-done
  121.4 0.0 copy-start.2
  121.4 1.0 copy.15
  122.4 0.1 copy-done.2
  122.4 0.0 copy-start.1
  122.4 0.7 copy.16
  123.1 0.3 copy-done.1
  123.4 0.7 copy.17
Async XLA Ops:
  119.0 2.4 %copy-start = (bf16[256,2048]{1,0:T(8,128)(2,1)S(1)}, bf16[256,2048]{1,0:T(8,128)(2,1)}, u32[]{:S(2)}) copy-start(bf16[256,2048]{1,0:T(8,128)(2,1)} %get-tuple-element.9) | copy-start | bytes 3145732
  121.4 1.0 copy-start.2
  122.4 1.0 copy-start.1

commit v7 on v4

--- a/solution.py
+++ b/solution.py
@@ -178,31 +178,32 @@
             x_c(zi, yi).wait_recv()
             g_c(zi, yi).wait_recv()
 
-    def middle(zi):
-        rows = pl.ds(zi * SLAB, SLAB)
+    def middle(zi, n):
+        rows = pl.ds(zi * SLAB, n * SLAB)
         pre = jnp.dot(X[rows, :], Wu[...], preferred_element_type=F32)
         back = lax.dot_general(G[rows, :], Wd[...], (((1,), (1,)), ((), ())), preferred_element_type=F32)
         s = jax.nn.sigmoid(pre)
         act = pre * s
         dpre = back * s * (1.0 + pre * (1.0 - s))
-        dT[...] = dpre.astype(BF16).T
-        aT[...] = act.astype(BF16).T
-
-    def grads(zi):
-        rows = pl.ds(zi * SLAB, SLAB)
+        dT[:, : n * SLAB] = dpre.astype(BF16).T
+        aT[:, : n * SLAB] = act.astype(BF16).T
+
+    def grads(zi, n):
+        rows = pl.ds(zi * SLAB, n * SLAB)
 
         @pl.loop(0, D // 256)
         def _(j):
             cols = pl.ds(pl.multiple_of(j * 256, 256), 256)
-            du = jnp.dot(dT[...], X[rows, cols], preferred_element_type=F32)
-            dd = jnp.dot(aT[...], G[rows, cols], preferred_element_type=F32)
+            du = jnp.dot(dT[:, : n * SLAB], X[rows, cols], preferred_element_type=F32)
+            dd = jnp.dot(aT[:, : n * SLAB], G[rows, cols], preferred_element_type=F32)
             accU[:, cols] = du if zi == 0 else accU[:, cols] + du
             accD[:, cols] = dd if zi == 0 else accD[:, cols] + dd
 
-    def unit(zi):
-        from_core(zi)
-        middle(zi)
-        grads(zi)
+    def unit(zi, n):
+        for i in range(n):
+            from_core(zi + i)
+        middle(zi, n)
+        grads(zi, n)
 
     for k in (1, 2, 3):
         long, short = 2 * k - 1, 2 * k
@@ -211,15 +212,13 @@
         if k < 3:
             pass_note(2 * k + 1)
         if k == 3:
-            unit(1)
+            unit(1, 2)
         arrived_g(long, 0, True, to_long)
         arrived_g(short, 0, k < 3, to_short)
-        if k == 3:
-            unit(2)
         arrived_pair(long)
         arrived_pair(short)
         if k == 3:
-            unit(3)
+            unit(3, 2)
         arrived_g(long, 1, True, to_long)
         arrived_g(short, 1, k < 3, to_short)
         if k < 3:
@@ -238,18 +237,15 @@
                 for c in w_send:
                     c.wait_recv()
 
-            unit(0)
-        if k == 3:
-            unit(4)
+            unit(0, 1)
 
     arrived_x(7, False, to_long)
-    unit(5)
     arrived_g(7, 0, False, to_long)
-    unit(6)
+    unit(5, 2)
     arrived_pair(7)
     arrived_g(7, 1, False, to_long)
     from_core(7)
-    middle(7)
+    middle(7, 1)
 
     last = pl.ds(7 * SLAB, SLAB)
     H4 = Q4 // 2
@@ -263,10 +259,10 @@
         return pl.ds(pl.multiple_of(((x + step) % 4) * Q4 + half[i] * H4, H4), H4)
 
     def total_up(m, at):
-        return accU[hidden(m), at] + jnp.dot(dT[hidden(m), :], X[last, at], preferred_element_type=F32)
+        return accU[hidden(m), at] + jnp.dot(dT[hidden(m), :SLAB], X[last, at], preferred_element_type=F32)
 
     def total_dn(m, at):
-        return accD[hidden(m), at] + jnp.dot(aT[hidden(m), :], G[last, at], preferred_element_type=F32)
+        return accD[hidden(m), at] + jnp.dot(aT[hidden(m), :SLAB], G[last, at], preferred_element_type=F32)
 
     def x_sum(m, i, n):
         return remote(
@@ -500,7 +496,7 @@
             vmem((8 * SLAB, D), BF16), vmem((8 * SLAB, D), BF16),
             vmem((D, FL), BF16), vmem((FL, D), BF16),
             vmem((FL, D), F32), vmem((FL, D), F32),
-            vmem((FL, SLAB), BF16), vmem((FL, SLAB), BF16),
+            vmem((FL, 2 * SLAB), BF16), vmem((FL, 2 * SLAB), BF16),
             vmem((2, 2, 6, FL // 2, Q4 // 2), BF16), vmem((2, 2, 6, FL // 2, Q4 // 2), BF16),
             vmem((2, 2, 2, 2, FL // 2, 128), BF16), vmem((2, 2, 2, FL // 2, 128), BF16),
             vmem((2, 2, 2, FL // 2, 128), BF16), vmem((2, 2, 2, FL // 2, 128), BF16),

time: 125 us -> 125 us (level)
  the two profiles are of different devices: /device:TPU:1 before, /device:TPU:33 now
where the time goes in v7:
time: 125 us
  Pallas kernels  119 us (95%)
  local copies, waits for them, and re-layouts  4.98 us (4%)
    pallas_call x1, Pallas kernels, local(): pl.pallas_call(outer_round, out_shape=(jax.ShapeDtypeStruct(up_weight.sha...  119 us
    unnamed x10, local copies, waits for them, and re-layouts  4.98 us

profile of v7, /device:TPU:33, one launch (start us, length us, event | category | flops | bytes accessed | tf_op | source)
XLA Modules:
  0.0 124.8 jit_solution(14656222791644000262)
XLA Ops:
  0.6 119.2 %outer_round.1 = (bf16[2048,256]{1,0:T(8,128)(2,1)}, bf16[256,2048]{1,0:T(8,128)(2,1)}, f32[128,256]{1,0:T(8,128)}, f32[256,128]{1,0:T(8,128)}) custom-call(bf16[48,2048]{1,0:T(8,128)(2,1)} %bitcast.2, bf16[48,2048]{1,0:T(8,128)(2,1)} %bitcast.3, bf16[2048,256]{1,0:T(8,128)(2,1)} %up.1, bf16[256,2048]{1,0:T(8,128)(2,1)} %down.1, f32[128,256]{1,0:T(8,128)} %mu.1, ...), custom_call_target="tpu_custom_call" | custom-call | tf_op jit(solution)/shard_map/outer_round/pallas_call | solution.py:485
  119.8 0.0 copy-start
  119.8 2.4 %copy.14 = bf16[2048,256]{1,0:T(8,128)(2,1)} copy(bf16[2048,256]{1,0:T(8,128)(2,1)} %get-tuple-element.8) | data formatting | bytes 2097152
  122.2 0.0 copy-done
  122.2 0.0 copy-start.2
  122.2 1.0 copy.15
  123.1 0.1 copy-done.2
  123.2 0.0 copy-start.1
  123.2 0.7 copy.16
  123.8 0.3 copy-done.1
  124.1 0.7 copy.17
Async XLA Ops:
  119.8 2.4 %copy-start = (bf16[256,2048]{1,0:T(8,128)(2,1)S(1)}, bf16[256,2048]{1,0:T(8,128)(2,1)}, u32[]{:S(2)}) copy-start(bf16[256,2048]{1,0:T(8,128)(2,1)} %get-tuple-element.9) | copy-start | bytes 3145732
  122.2 1.0 copy-start.2
  123.2 1.0 copy-start.1
